TPU v7x, 32 devices: a whole 2x2x4 slice. The times are simulated.
32 devices in a mesh: grp: 4 (over x, core), seq: 8 (over z, y).
Axes of the slice: x: 2, y: 2, z: 4, core: 2. Of those that a mesh axis runs over, the one named last changes fastest.
Arguments:
- tokens: bfloat16 [16, 4, 5120], P(None, None, ('grp', 'seq')), may hold values from -90 to 90
- lengths: int32 [16], replicated, may hold values from 1 to 8192, as said below
- group_perm: int32 [16], replicated, may hold values from 0 to 15, as said below
- page_table: int32 [16, 64], replicated, may hold values from 0 to 31, as said below
- k_pool: bfloat16 [1024, 128, 1024], P(('grp', 'seq')), may hold values from -17 to 17
- v_pool: bfloat16 [1024, 128, 1024], P(('grp', 'seq')), may hold values from -7 to 7
- gain_in: float32 [5120], P(('grp', 'seq')), may hold values from 0.25 to 1.75
- qkv_weight: bfloat16 [5120, 7168], P('grp', 'seq'), may hold values from -0.15625 to 0.15625
- qkv_bias: float32 [7168], P('seq'), may hold values from -16 to 16
- o_weight: bfloat16 [5120, 5120], P('seq', 'grp'), may hold values from -0.078125 to 0.078125
- gain_mid: float32 [5120], P(('grp', 'seq')), may hold values from 0.25 to 1.75
- gate_weight: bfloat16 [5120, 13824], P('grp', 'seq'), may hold values from -0.078125 to 0.078125
- up_weight: bfloat16 [5120, 13824], P('grp', 'seq'), may hold values from -0.078125 to 0.078125
- down_weight: bfloat16 [13824, 5120], P('seq', 'grp'), may hold values from -0.0546875 to 0.0546875
Outputs:
- mixed: bfloat16 [16, 4, 5120], P(None, None, ('grp', 'seq'))
Inputs may be any that keep to these rules, and one draw needn't show every extreme that they name: `lengths`: one request holds exactly 8192 cached tokens. A permutation of the requests; request group_perm[i] belongs to group i // 4. `page_table`: page p of request r lies on the device with grp index g and seq index p // 8, where g is the group of r; the slots named for one device are all different.
All inputs are finite; a program needn't handle non-finite values.
Results may differ from a plain program's by a relative error of at most 0.015.
Values may be sent and summed in bfloat16 or wider, within the bound.
A program may use at most 128 MiB of HBM per device.

v0:
```python
import jax
import jax.numpy as jnp
from jax import lax
from jax.sharding import PartitionSpec as P

D = 5120
HEADS = 40
KV_HEADS = 8
HEAD_DIM = 128
STEPS = 4
REQ_GRP = 4
SHARD_PAGES = 8
PAGE = 128
BLOCK_PAGES = 4


EPSILON = 1e-06
LOW_SCORE = -1e30
ROPE_BASE = 1000000.0


def rotary(values, position):
    half_dim = values.shape[-1] // 2
    exponent = jnp.arange(half_dim, dtype=jnp.float32) * (2.0 / values.shape[-1])
    inverse = jnp.exp(-exponent * jnp.log(jnp.float32(ROPE_BASE)))
    angle = position[..., None, None] * inverse
    cosine = jnp.cos(angle)
    sine_part = jnp.sin(angle)
    first_half = values[..., :half_dim]
    second_half = values[..., half_dim:]
    return jnp.concatenate(
        [
            first_half * cosine - second_half * sine_part,
            second_half * cosine + first_half * sine_part,
        ],
        axis=-1,
    )


def absorb(carried, query_mat, key_block, value_block, live_mask, score_scale):
    best_score, weight_sums, weighted = carried
    scores = (
        jnp.einsum("hqd,khd->hqk", query_mat, key_block, preferred_element_type=jnp.float32)
        * score_scale
    )
    scores = jnp.where(live_mask, scores, LOW_SCORE)
    fresh_top = jnp.maximum(best_score, jnp.max(scores, axis=-1))
    rescale = jnp.exp(best_score - fresh_top)
    weights = jnp.where(live_mask, jnp.exp(scores - fresh_top[..., None]), 0.0)
    weight_sums = weight_sums * rescale + jnp.sum(weights, axis=-1)
    weighted = weighted * rescale[..., None] + jnp.einsum(
        "hqk,khd->hqd",
        weights.astype(jnp.bfloat16),
        value_block,
        preferred_element_type=jnp.float32,
    )
    return (fresh_top, weight_sums, weighted)


def body(
    tokens,
    lengths,
    group_perm,
    page_table,
    k_pool,
    v_pool,
    gain_in,
    qkv_weight,
    qkv_bias,
    o_weight,
    gain_mid,
    gate_weight,
    up_weight,
    down_weight,
):
    n_seq = lax.axis_size("seq")
    grp_idx = lax.axis_index("grp")
    seq_idx = lax.axis_index("seq")
    group_q = HEADS // KV_HEADS
    query_rows = STEPS * group_q
    q_width = HEADS * HEAD_DIM
    kv_width = KV_HEADS * HEAD_DIM
    score_scale = HEAD_DIM ** (-0.5)
    sorted_rows = jnp.take(tokens, group_perm, axis=0).astype(jnp.float32)
    squares_in = lax.psum(jnp.sum(sorted_rows * sorted_rows, axis=-1), ("grp", "seq"))
    normed_in = (sorted_rows * lax.rsqrt(squares_in / D + EPSILON)[..., None] * gain_in).astype(
        jnp.bfloat16
    )
    proj_part = jnp.einsum(
        "rtc,ck->rtk",
        lax.all_gather(normed_in, "seq", axis=2, tiled=True),
        qkv_weight,
        preferred_element_type=jnp.float32,
    )
    proj_share = (
        lax.psum_scatter(
            proj_part.astype(jnp.bfloat16), "grp", scatter_dimension=0, tiled=True
        ).astype(jnp.float32)
        + qkv_bias
    )
    proj_full = lax.all_gather(proj_share, "seq", axis=2, tiled=True)
    members = lax.dynamic_slice_in_dim(group_perm, grp_idx * REQ_GRP, REQ_GRP)
    my_lengths = jnp.take(lengths, members)
    steps_range = jnp.arange(STEPS, dtype=jnp.int32)
    position = (my_lengths[:, None] + steps_range[None, :]).astype(jnp.float32)
    queries = rotary(
        proj_full[..., :q_width].reshape(REQ_GRP, STEPS, HEADS, HEAD_DIM), position
    ).astype(jnp.bfloat16)
    new_keys = rotary(
        proj_full[..., q_width : q_width + kv_width].reshape(REQ_GRP, STEPS, KV_HEADS, HEAD_DIM),
        position,
    ).astype(jnp.bfloat16)
    new_values = (
        proj_full[..., q_width + kv_width :]
        .reshape(REQ_GRP, STEPS, KV_HEADS, HEAD_DIM)
        .astype(jnp.bfloat16)
    )
    shard_rows = SHARD_PAGES * PAGE
    block_rows = BLOCK_PAGES * PAGE
    shard_base = seq_idx * shard_rows
    slot_table = lax.dynamic_slice_in_dim(
        jnp.take(page_table, members, axis=0), seq_idx * SHARD_PAGES, SHARD_PAGES, 1
    )
    is_last = seq_idx == n_seq - 1
    causal = (
        steps_range[None, :] <= (jnp.arange(query_rows, dtype=jnp.int32) // group_q)[:, None]
    ) & is_last
    causal = causal[None]
    query_all = (
        queries.reshape(REQ_GRP, STEPS, KV_HEADS, group_q, HEAD_DIM)
        .transpose(0, 2, 1, 3, 4)
        .reshape(REQ_GRP, KV_HEADS, query_rows, HEAD_DIM)
    )
    live_all = jnp.clip(my_lengths - shard_base, 0, shard_rows)
    block_offsets = jnp.arange(block_rows, dtype=jnp.int32)
    initial = (
        jnp.full((REQ_GRP, KV_HEADS, query_rows), LOW_SCORE, jnp.float32),
        jnp.zeros((REQ_GRP, KV_HEADS, query_rows), jnp.float32),
        jnp.zeros((REQ_GRP, KV_HEADS, query_rows, HEAD_DIM), jnp.float32),
    )
    absorb_all = jax.vmap(absorb, in_axes=(0, 0, 0, 0, None, None))
    carried = absorb_all(initial, query_all, new_keys, new_values, causal, score_scale)
    absorb_masked = jax.vmap(absorb, in_axes=(0, 0, 0, 0, 0, None))
    block_count = (jnp.max(live_all) + block_rows - 1) // block_rows

    def advance_all(block_index, running):
        slot_ids = lax.dynamic_slice_in_dim(slot_table, block_index * BLOCK_PAGES, BLOCK_PAGES, 1)
        key_block = jnp.take(k_pool, slot_ids.reshape(-1), axis=0).reshape(
            REQ_GRP, block_rows, KV_HEADS, HEAD_DIM
        )
        value_block = jnp.take(v_pool, slot_ids.reshape(-1), axis=0).reshape(
            REQ_GRP, block_rows, KV_HEADS, HEAD_DIM
        )
        positions = shard_base + block_index * block_rows + block_offsets
        live_mask = (positions[None, :] < my_lengths[:, None])[:, None, None, :]
        return absorb_masked(running, query_all, key_block, value_block, live_mask, score_scale)

    best_score, weight_sums, weighted = lax.fori_loop(0, block_count, advance_all, carried)
    top_score = lax.pmax(best_score, "seq")
    factor = jnp.exp(best_score - top_score)
    weight_sums, weighted = (
        lax.psum((weight_sums * factor).astype(jnp.bfloat16), "seq").astype(jnp.float32),
        lax.psum((weighted * factor[..., None]).astype(jnp.bfloat16), "seq").astype(jnp.float32),
    )
    attended = (weighted / weight_sums[..., None]).reshape(
        REQ_GRP, KV_HEADS, STEPS, group_q, HEAD_DIM
    )
    attended = (
        attended.transpose(0, 2, 1, 3, 4).reshape(REQ_GRP, STEPS, q_width).astype(jnp.bfloat16)
    )
    out_width = o_weight.shape[0]
    attended_cols = lax.dynamic_slice_in_dim(attended, seq_idx * out_width, out_width, 2)
    out_terms = jnp.einsum(
        "rtc,cd->rtd",
        lax.all_gather(attended_cols, "grp", axis=0, tiled=True),
        o_weight,
        preferred_element_type=jnp.float32,
    )
    attn_sum = lax.psum_scatter(
        out_terms.astype(jnp.bfloat16), "seq", scatter_dimension=2, tiled=True
    ).astype(jnp.float32)
    residual = sorted_rows + attn_sum
    squares_mid = lax.psum(jnp.sum(residual * residual, axis=-1), ("grp", "seq"))
    normed_mid = (residual * lax.rsqrt(squares_mid / D + EPSILON)[..., None] * gain_mid).astype(
        jnp.bfloat16
    )
    segment = lax.all_gather(normed_mid, "seq", axis=2, tiled=True)
    gate_part = jnp.einsum("rtc,cf->rtf", segment, gate_weight, preferred_element_type=jnp.float32)
    up_part = jnp.einsum("rtc,cf->rtf", segment, up_weight, preferred_element_type=jnp.float32)
    gate_sum, up_sum = (
        lax.psum(gate_part.astype(jnp.bfloat16), "grp").astype(jnp.float32),
        lax.psum(up_part.astype(jnp.bfloat16), "grp").astype(jnp.float32),
    )
    hidden = (jax.nn.silu(gate_sum) * up_sum).astype(jnp.bfloat16)
    down_terms = jnp.einsum("rtf,fd->rtd", hidden, down_weight, preferred_element_type=jnp.float32)
    down_sum = lax.psum_scatter(
        down_terms.astype(jnp.bfloat16), "seq", scatter_dimension=2, tiled=True
    ).astype(jnp.float32)
    restore = jnp.argsort(group_perm)
    return jnp.take(residual + down_sum, restore, axis=0).astype(jnp.bfloat16)


def solution(mesh):
    return jax.shard_map(
        body,
        mesh=mesh,
        in_specs=(
            P(None, None, ("grp", "seq")),
            P(),
            P(),
            P(),
            P(("grp", "seq"), None, None),
            P(("grp", "seq"), None, None),
            P(("grp", "seq")),
            P("grp", "seq"),
            P("seq"),
            P("seq", "grp"),
            P(("grp", "seq")),
            P("grp", "seq"),
            P("grp", "seq"),
            P("seq", "grp"),
        ),
        out_specs=P(None, None, ("grp", "seq")),
        check_vma=False,
    )
```

profile of v0, /device:TPU:0, one launch (start us, length us, event | category | flops | bytes accessed | tf_op | source)
XLA Modules:
  0.0 582.3 jit_solution(14660089544328055868)
XLA Ops:
  6.6 2.0 sort.17
  8.6 0.7 compare_select_fusion.2
  9.3 0.7 compare_and_fusion.2
  9.9 1.4 gather_fusion.2
  11.3 0.2 fusion.54
  11.5 42.0 %psum.42 = f32[16,4]{0,1:T(4,128)S(1)} all-reduce(f32[16,4]{0,1:T(4,128)S(1)} %fusion.54), channel_id=1, replica_groups=mesh['grp'=4,'seq'=8] {'grp','seq'}, use_global_device_ids=true, to_apply=%region_2.3 | all-reduce | flops 64 | bytes 512 | tf_op jit(solution)/shard_map/psum | solution.py:85
  53.5 0.8 fusion.56
  54.3 0.2 copy.89
  54.4 35.1 %all_gather.12 = bf16[16,4,1280]{0,1,2:T(4,128)(2,1)S(1)} all-gather(bf16[16,4,160]{0,1,2:T(4,128)(2,1)S(1)} %copy.89), channel_id=1, replica_groups=mesh['grp'=4,'seq'=8] {'seq'}, dimensions={2}, use_global_device_ids=true | all-gather | bytes 184320 | tf_op jit(solution)/shard_map/all_gather | solution.py:91
  89.5 1.2 fusion.39
  91.0 0.6 gather_fusion.3
  91.6 0.6 clamp_reduce_fusion
  93.0 0.6 gather_fusion.4
  93.7 0.6 dynamic-slice
  95.0 25.0 %all-reduce.8.cloned.1.call-done = bf16[16,4,896]{2,0,1:T(8,128)(2,1)} async-done(((bf16[16,4,896]{2,0,1:T(8,128)(2,1)}), bf16[16,4,896]{2,0,1:T(8,128)(2,1)}) %all-reduce.8.cloned.1.call-update) | async-done | bytes 114704
  120.0 0.8 convert_add_fusion.2
  120.9 31.3 %all_gather.13 = f32[4,4,7168]{2,0,1:T(4,128)S(1)} all-gather(f32[4,4,896]{2,0,1:T(4,128)S(1)} %convert_add_fusion.2), channel_id=1, replica_groups=mesh['grp'=4,'seq'=8] {'seq'}, dimensions={2}, use_global_device_ids=true | all-gather | bytes 516096 | tf_op jit(solution)/shard_map/all_gather | solution.py:101
  152.6 0.4 subtract_convert_fusion
  153.0 0.2 maximum_bitcast_fusion
  153.6 0.3 fusion.75
  154.0 0.3 convolution_add_fusion
  154.3 58.6 %while.15 = (s32[]{:T(128)}, f32[4,8,20]{2,1,0:T(8,128)S(1)}, f32[4,8,20]{2,1,0:T(8,128)S(1)}, f32[4,8,20,128]{3,2,1,0:T(8,128)S(1)}, s32[]{:T(128)}, /*index=5*...) while((s32[]{:T(128)}, f32[4,8,20]{2,1,0:T(8,128)S(1)}, ...), condition=%wide.region_10.12_spmd.clone, body=%wide.region_7.11_spmd.clone.sunk | while | flops 175084448 | bytes 80307120 | solution.py:158
  154.5 6.2 %gather_fusion = bf16[16,128,1024]{2,1,0:T(8,128)(2,1)} fusion(bf16[32,128,1024]{2,1,0:T(8,128)(2,1)} %get-tuple-element.321, s32[1024]{0:T(1024)S(1)} %pad_clamp_fusion.5), kind=kCustom, calls=%fused_computation.1.clone.clone.1 | custom fusion | bytes 8388672 | tf_op jit(solution)/shard_map/while/body/jit(_take)/gather | solution.py:151
  160.7 6.1 %gather_fusion.1 = bf16[16,128,1024]{2,1,0:T(8,128)(2,1)} fusion(bf16[32,128,1024]{2,1,0:T(8,128)(2,1)} %get-tuple-element.319, s32[1024]{0:T(1024)S(1)} %pad_clamp_fusion.5), kind=kCustom, calls=%fused_computation.clone.clone.1 | custom fusion | bytes 8388672 | tf_op jit(solution)/shard_map/while/body/jit(_take)/gather | solution.py:148
  166.8 6.2 %broadcast_select_fusion.6 = (bf16[16,128,1024]{2,1,0:T(8,128)(2,1)}, bf16[16,128,1024]{2,1,0:T(8,128)(2,1)S(1)}) fusion(bf16[16,128,1024]{2,1,0:T(8,128)(2,1)} %gather_fusion, pred[16]{0:T(512)(128)(4,1)S(1)} %compare_and_fusion.5, bf16[16,128,1024]{2,1,0:T(8,128)(2,1)} %gather_fusion.1), kind=kLoop, calls=%fused_computation.11.clone.1 | loop fusion | flops 4194304 | bytes 16777232 | tf_op jit(solution)/shard_map/while/body/jit(_take)/select_n | solution.py:151
  173.1 3.0 copy.177
  176.2 4.7 bitcast_reduce_fusion.2
  180.9 0.5 fusion.87
  181.4 1.1 copy.178
  182.5 1.1 fusion.88
  183.8 6.2 %gather_fusion = bf16[16,128,1024]{2,1,0:T(8,128)(2,1)} fusion(bf16[32,128,1024]{2,1,0:T(8,128)(2,1)} %get-tuple-element.321, s32[1024]{0:T(1024)S(1)} %pad_clamp_fusion.5), kind=kCustom, calls=%fused_computation.1.clone.clone.1 | custom fusion | bytes 8388672 | tf_op jit(solution)/shard_map/while/body/jit(_take)/gather | solution.py:151
  190.0 6.1 %gather_fusion.1 = bf16[16,128,1024]{2,1,0:T(8,128)(2,1)} fusion(bf16[32,128,1024]{2,1,0:T(8,128)(2,1)} %get-tuple-element.319, s32[1024]{0:T(1024)S(1)} %pad_clamp_fusion.5), kind=kCustom, calls=%fused_computation.clone.clone.1 | custom fusion | bytes 8388672 | tf_op jit(solution)/shard_map/while/body/jit(_take)/gather | solution.py:148
  196.1 6.2 %broadcast_select_fusion.6 = (bf16[16,128,1024]{2,1,0:T(8,128)(2,1)}, bf16[16,128,1024]{2,1,0:T(8,128)(2,1)S(1)}) fusion(bf16[16,128,1024]{2,1,0:T(8,128)(2,1)} %gather_fusion, pred[16]{0:T(512)(128)(4,1)S(1)} %compare_and_fusion.5, bf16[16,128,1024]{2,1,0:T(8,128)(2,1)} %gather_fusion.1), kind=kLoop, calls=%fused_computation.11.clone.1 | loop fusion | flops 4194304 | bytes 16777232 | tf_op jit(solution)/shard_map/while/body/jit(_take)/select_n | solution.py:151
  202.4 3.0 copy.177
  205.4 4.7 bitcast_reduce_fusion.2
  210.2 0.5 fusion.87
  210.7 1.1 copy.178
  211.8 1.1 fusion.88
  212.9 37.1 %pmax.7 = f32[4,8,20]{2,1,0:T(8,128)S(1)} all-reduce(f32[4,8,20]{2,1,0:T(8,128)S(1)} %get-tuple-element.74), channel_id=1, replica_groups=mesh['grp'=4,'seq'=8] {'seq'}, use_global_device_ids=true, to_apply=%region_11.13 | all-reduce | flops 640 | bytes 5120 | tf_op jit(solution)/shard_map/pmax | solution.py:159
  250.1 0.8 fusion.50
  251.0 17.4 %psum.44 = bf16[4,8,20]{2,1,0:T(8,128)(2,1)S(1)} all-reduce(bf16[4,8,20]{2,1,0:T(8,128)(2,1)S(1)} %get-tuple-element.171), channel_id=1, replica_groups=mesh['grp'=4,'seq'=8] {'seq'}, use_global_device_ids=true, to_apply=%region_13.15 | all-reduce | flops 640 | bytes 2560 | tf_op jit(solution)/shard_map/psum | solution.py:162
  268.5 47.8 %all-reduce.6.cloned.1.call-done = bf16[4,8,20,128]{3,1,2,0:T(8,128)(2,1)} async-done(((bf16[4,8,20,128]{3,1,2,0:T(8,128)(2,1)}), bf16[4,8,20,128]{3,1,2,0:T(8,128)(2,1)}) %all-reduce.6.cloned.1.call-update) | async-done | bytes 163856 | tf_op jit(solution)/shard_map/psum | solution.py:163
  316.4 1.1 divide_convert_fusion
  317.7 5.3 all_gather.14
  323.0 1.8 convolution_convert_fusion
  324.7 0.8 copy.117
  325.5 1.4 reshape.220
  327.0 61.2 %reduce-scatter.8.cloned.1.call-done = bf16[160,64]{1,0:T(8,128)(2,1)} async-done(((bf16[1280,64]{1,0:T(8,128)(2,1)}), bf16[160,64]{1,0:T(8,128)(2,1)}) %reduce-scatter.8.cloned.1.call-update) | async-done | bytes 20496
  388.1 0.9 reshape.221
  389.1 0.2 multiply_reduce_fusion
  389.3 40.2 %psum.45 = f32[16,4]{0,1:T(4,128)S(1)} all-reduce(f32[16,4]{0,1:T(4,128)S(1)} %multiply_reduce_fusion), channel_id=1, replica_groups=mesh['grp'=4,'seq'=8] {'grp','seq'}, use_global_device_ids=true, to_apply=%region_16.18 | all-reduce | flops 64 | bytes 512 | tf_op jit(solution)/shard_map/psum | solution.py:183
  429.6 0.2 copy.106
  429.8 34.9 %all_gather.15 = bf16[16,4,1280]{0,1,2:T(4,128)(2,1)S(1)} all-gather(bf16[16,4,160]{0,1,2:T(4,128)(2,1)S(1)} %copy.106), channel_id=1, replica_groups=mesh['grp'=4,'seq'=8] {'seq'}, dimensions={2}, use_global_device_ids=true | all-gather | bytes 184320 | tf_op jit(solution)/shard_map/all_gather | solution.py:187
  464.6 0.7 copy.107
  465.4 4.5 fusion.26
  469.9 2.1 fusion.29
  472.1 31.8 %all-reduce.10.cloned.1.call-done = (bf16[16,4,1728]{2,0,1:T(8,128)(2,1)}, bf16[16,4,1728]{2,0,1:T(8,128)(2,1)}) async-done(((bf16[16,4,1728]{2,0,1:T(8,128)(2,1)}, bf16[16,4,1728]{2,0,1:T(8,128)(2,1)}), (bf16[16,4,1728]{2,0,1:T(8,128)(2,1)}, bf16[16,4,1728]{2,0,1:T(8,128)(2,1)})) %all-reduce.10.cloned.1.call-update) | async-done | bytes 442384 | tf_op jit(solution)/shard_map/psum | solution.py:192
  503.9 3.5 fusion.32
  507.4 1.5 copy.119
  509.0 2.7 reshape.222
  511.7 61.6 %reduce-scatter.10.cloned.1.call-done = bf16[160,64]{1,0:T(8,128)(2,1)} async-done(((bf16[1280,64]{1,0:T(8,128)(2,1)}), bf16[160,64]{1,0:T(8,128)(2,1)}) %reduce-scatter.10.cloned.1.call-update) | async-done | bytes 20496
  573.4 0.9 reshape.223
  574.5 0.6 gather_fusion.5
  575.1 0.7 select_convert_fusion
  (94 shorter events, 2.9 us)
Async XLA Ops:
  6.5 83.0 %copy-start = (bf16[1280,896]{1,0:T(8,128)(2,1)S(1)}, bf16[1280,896]{1,0:T(8,128)(2,1)}, u32[]{:S(2)}) copy-start(bf16[1280,896]{1,0:T(8,128)(2,1)} %param.25) | copy-start | bytes 6881284
  6.5 84.3 %copy-start.5 = (s32[16]{0:T(128)S(1)}, s32[16]{0:T(128)}, u32[]{:S(2)}) copy-start(s32[16]{0:T(128)} %param.20) | copy-start | bytes 196
  6.5 84.4 %copy-start.2 = (s32[16]{0:T(128)S(1)}, s32[16]{0:T(128)}, u32[]{:S(2)}) copy-start(s32[16]{0:T(128)} %param.19) | copy-start | bytes 196
  6.5 113.5 %all-reduce.8.cloned.1.call-start = ((), (), s32[]{:S(2)}) async-start(), calls=%async_computation.5 | async-start | bytes 229376
  11.3 81.7 %copy-start.4 = (s32[16,64]{1,0:T(8,128)S(1)}, s32[16,64]{1,0:T(8,128)}, u32[]{:S(2)}) copy-start(s32[16,64]{1,0:T(8,128)} %param.21) | copy-start | bytes 12292
  53.5 40.2 %copy-start.8 = (u32[32]{0:T(128)S(1)}, u32[32]{0:T(128)}, u32[]{:S(2)}) copy-start(u32[32]{0:T(128)} %constant.159) | copy-start | bytes 388
  54.3 65.8 %copy-start.6 = (f32[896]{0:T(1024)S(1)}, f32[896]{0:T(1024)}, u32[]{:S(2)}) copy-start(f32[896]{0:T(1024)} %param.26) | copy-start | bytes 10756
  90.8 225.6 %all-reduce.6.cloned.1.call-start = ((), (), s32[]{:S(2)}) async-start(), calls=%async_computation.2 | async-start | bytes 327680 | tf_op jit(solution)/shard_map/psum | solution.py:163
  176.2 5.2 copy-start.3
  205.4 5.2 copy-start.3
  212.9 216.6 %copy-start.7 = (f32[160]{0:T(256)S(1)}, f32[160]{0:T(256)}, u32[]{:S(2)}) copy-start(f32[160]{0:T(256)} %param.28) | copy-start | bytes 1924
  250.9 137.2 %reduce-scatter.8.cloned.1.call-start = ((), (), s32[]{:S(2)}) async-start(), calls=%async_computation.3 | async-start | bytes 368640
  326.9 177.0 %all-reduce.10.cloned.1.call-start = ((), (), s32[]{:S(2)}) async-start(), calls=%async_computation.6 | async-start | bytes 917504 | tf_op jit(solution)/shard_map/psum | solution.py:192
  464.6 5.2 slice-start
  465.3 4.5 slice-start.1
  472.0 101.3 %reduce-scatter.10.cloned.1.call-start = ((), (), s32[]{:S(2)}) async-start(), calls=%async_computation.4 | async-start | bytes 368640
  503.9 71.9 %copy-start.1 = (bf16[1280,896]{1,0:T(8,128)(2,1)S(1)}, bf16[1280,896]{1,0:T(8,128)(2,1)}, u32[]{:S(2)}) copy-start(bf16[1280,896]{1,0:T(8,128)(2,1)} %param.25) | copy-start | bytes 6881284
Sparse Core Ops, SparseCore 0:
  90.9 29.1 all-reduce.7
  251.1 65.2 all-reduce.5
  327.0 61.0 reduce-scatter.7
  472.2 31.7 all-reduce.9
  511.9 61.4 reduce-scatter.9
where the time goes:
time: 584 us; the launch traced here: 582 us
  blocking collectives  243 us (42%)
  waiting for transfers between devices  228 us (39%)
  local copies, waits for them, and re-layouts  47.4 us (8%)
  matrix products  25.4 us (4%)
  other arithmetic  23.7 us (4%)
  between operations  14.8 us (3%)
    unnamed x8, waiting for transfers between devices  148 us
    psum x1, waiting for transfers between devices, body(): lax.psum((weighted * factor[..., None]).astype(jnp.bfloat16), 'seq')  47.8 us
    psum x1, blocking collectives, body(): lax.psum(jnp.sum(sorted_rows * sorted_rows, axis=-1), ('grp', 'seq'))  42 us
    psum x1, blocking collectives, body(): lax.psum(jnp.sum(residual * residual, axis=-1), ('grp', 'seq'))  40.2 us
    pmax x1, blocking collectives, body(): top_score = lax.pmax(best_score, 'seq')  37.1 us
    all_gather x1, blocking collectives, body(): lax.all_gather(normed_in, 'seq', axis=2, tiled=True)  35.1 us
    all_gather x1, blocking collectives, body(): segment = lax.all_gather(normed_mid, 'seq', axis=2, tiled=True)  34.9 us
    psum x1, waiting for transfers between devices, body(): lax.psum(up_part.astype(jnp.bfloat16), 'grp').astype(jnp.float32)  31.8 us
  transfers between devices with their start and end apart: 5, of which 5 were waited for; matrix products, arithmetic and copies ran while one was open for 1% of the time, Pallas kernels for 0%

commit v1 on v0

--- a/solution.py
+++ b/solution.py
@@ -1,6 +1,10 @@
+import functools
+
 import jax
 import jax.numpy as jnp
 from jax import lax
+from jax.experimental import pallas as pl
+from jax.experimental.pallas import tpu as pltpu
 from jax.sharding import PartitionSpec as P
 
 D = 5120
@@ -200,9 +204,492 @@
     return jnp.take(residual + down_sum, restore, axis=0).astype(jnp.bfloat16)
 
 
+N_GRP = 4
+N_SEQ = 8
+ROWS = 64
+GROWS = REQ_GRP * STEPS
+FEAT = D // (N_GRP * N_SEQ)
+FEAT_PAD = 256
+DEPTH = D // N_GRP
+GROUP_Q = HEADS // KV_HEADS
+QROWS = 32
+SHARD_ROWS = SHARD_PAGES * PAGE
+MESH = pl.DeviceIdType.MESH
+
+
+def stat_lanes(pieces, rows, at=0, width=128, base=None):
+    lane = lax.broadcasted_iota(jnp.int32, (rows, width), 1)
+    block = jnp.zeros((rows, width), jnp.float32) if base is None else base
+    for offset, piece in enumerate(pieces):
+        block = jnp.where(lane == at + offset, piece, block)
+    return block
+
+
+def split_bf16(value, count):
+    pieces = []
+    for _ in range(count):
+        piece = value.astype(jnp.bfloat16).astype(jnp.float32)
+        pieces.append(piece)
+        value = value - piece
+    return pieces
+
+
+def fused_kernel(
+    lengths,
+    group_perm,
+    page_table,
+    tokens,
+    gain_in,
+    qkv_bias,
+    gain_mid,
+    k_hbm,
+    v_hbm,
+    qkv_hbm,
+    o_hbm,
+    gate_hbm,
+    up_hbm,
+    down_hbm,
+    out,
+    k_pool,
+    v_pool,
+    w_qkv,
+    w_o,
+    w_gate,
+    w_up,
+    w_down,
+    x_all,
+    x_wide,
+    x_bf,
+    qkv_send,
+    qkv_recv,
+    heads_all,
+    q_pairs,
+    new_k,
+    new_v,
+    att_send,
+    att_recv,
+    att_all,
+    wide,
+    o_send,
+    o_recv,
+    mid_all,
+    ff_send,
+    ff_recv,
+    hid_all,
+    down_send,
+    down_recv,
+    load_sem,
+    send_sem,
+    recv_sem,
+):
+    g = lax.axis_index("grp")
+    s = lax.axis_index("seq")
+    f32, bf16 = jnp.float32, jnp.bfloat16
+
+    loads = [
+        pltpu.make_async_copy(src, dst, load_sem.at[i])
+        for i, (src, dst) in enumerate(
+            [
+                (qkv_hbm, w_qkv),
+                (k_hbm, k_pool),
+                (v_hbm, v_pool),
+                (o_hbm, w_o),
+                (gate_hbm, w_gate),
+                (up_hbm, w_up),
+                (down_hbm, w_down),
+            ]
+        )
+    ]
+    for load in loads:
+        load.start()
+    barrier = pltpu.get_barrier_semaphore()
+    for d in range(1, N_SEQ):
+        pl.semaphore_signal(
+            barrier, inc=1, device_id={"seq": lax.rem(s + d, N_SEQ)}, device_id_type=MESH
+        )
+    for d in range(1, N_GRP):
+        pl.semaphore_signal(
+            barrier, inc=1, device_id={"grp": lax.rem(g + d, N_GRP)}, device_id_type=MESH
+        )
+
+    def exchange(stage, axis, source, target):
+        me, count = (s, N_SEQ) if axis == "seq" else (g, N_GRP)
+        copies = []
+        for d in range(1, count):
+            peer = lax.rem(me + d, count)
+            copy = pltpu.make_async_remote_copy(
+                src_ref=source(peer),
+                dst_ref=target,
+                send_sem=send_sem.at[stage, d],
+                recv_sem=recv_sem.at[stage, d],
+                device_id={axis: peer},
+                device_id_type=MESH,
+            )
+            copy.start()
+            copies.append(copy)
+        return copies
+
+    def arrive(copies):
+        for copy in copies:
+            copy.wait_recv()
+
+    started = []
+
+    row_i = lax.broadcasted_iota(jnp.int32, (ROWS, ROWS), 0)
+    col_i = lax.broadcasted_iota(jnp.int32, (ROWS, ROWS), 1)
+    origin = jnp.zeros((ROWS, ROWS), jnp.int32)
+    for i in range(ROWS // STEPS):
+        origin = jnp.where(row_i // STEPS == i, group_perm[i], origin)
+    order = (
+        ((col_i // STEPS) == origin) & ((col_i % STEPS) == (row_i % STEPS))
+    ).astype(f32).astype(bf16)
+    sorted_rows = jnp.dot(order, tokens[...], preferred_element_type=f32)
+
+    def feature_block(values, gain):
+        squares = jnp.sum(values * values, axis=1, keepdims=True)
+        return stat_lanes(
+            split_bf16(squares, 2), ROWS, FEAT, FEAT_PAD, values * gain
+        ).astype(bf16)
+
+    x_all[s] = feature_block(sorted_rows, gain_in[...])
+    pl.semaphore_wait(barrier, N_SEQ + N_GRP - 2)
+
+    def gather_features(stage, blocks):
+        copies = exchange(stage, "seq", lambda peer: blocks.at[s], blocks.at[s])
+        started.extend(copies)
+        arrive(copies)
+        lane = lax.broadcasted_iota(jnp.int32, (ROWS, FEAT_PAD), 1)
+        x_wide[...] = jnp.zeros_like(x_wide)
+        squares = jnp.zeros((ROWS, 1), f32)
+        for i in range(N_SEQ):
+            block = blocks[i].astype(f32)
+            kept = jnp.where(lane < FEAT, block, 0.0)
+            squares = squares + jnp.sum(block - kept, axis=1, keepdims=True)
+            first = i * FEAT // 128 * 128
+            kept = jnp.concatenate([kept, jnp.zeros((ROWS, 128), f32)], axis=1)
+            if i * FEAT - first:
+                kept = pltpu.roll(kept, i * FEAT - first, 1)
+            x_wide[:, first : first + 384] += kept
+        x_bf[...] = x_wide[:, :DEPTH].astype(bf16)
+        return squares
+
+    squares_in = gather_features(0, x_all)
+
+    loads[0].wait()
+    part = jnp.dot(x_bf[...], w_qkv[...], preferred_element_type=f32).astype(bf16)
+    stats = stat_lanes(split_bf16(squares_in, 2), ROWS).astype(bf16)
+    for i in range(N_GRP):
+        rows = slice(i * GROWS, (i + 1) * GROWS)
+        qkv_send[i, :, :896] = part[rows]
+        qkv_send[i, :, 896:] = stats[rows]
+    copies = exchange(1, "grp", lambda peer: qkv_send.at[peer], qkv_recv.at[g])
+    started.extend(copies)
+    qkv_recv[g] = qkv_send[g]
+
+    row16 = lax.broadcasted_iota(jnp.int32, (GROWS, HEAD_DIM), 0)
+    lane16 = lax.broadcasted_iota(jnp.int32, (GROWS, HEAD_DIM), 1)
+    position = row16 % STEPS
+    for r in range(REQ_GRP):
+        length = lengths[group_perm[g * REQ_GRP + r]]
+        position = position + jnp.where(row16 // STEPS == r, length, 0)
+    half = HEAD_DIM // 2
+    exponent = (lane16 % half).astype(f32) * (2.0 / HEAD_DIM)
+    angle = position.astype(f32) * jnp.exp(-exponent * jnp.log(jnp.full((), ROPE_BASE, f32)))
+    cosine = jnp.cos(angle)
+    sine = jnp.where(lane16 < half, -jnp.sin(angle), jnp.sin(angle))
+
+    arrive(copies)
+    summed = sum(qkv_recv[i].astype(f32) for i in range(N_GRP))
+    scale = lax.rsqrt(jnp.sum(summed[:, 896:], axis=1, keepdims=True) / D + EPSILON)
+    share = summed[:, :896] * scale + qkv_bias[...]
+    per_dev = 896 // HEAD_DIM
+    for j in range(per_dev):
+        unit = share[:, j * HEAD_DIM : (j + 1) * HEAD_DIM]
+        turned = unit * cosine + pltpu.roll(unit, half, 1) * sine
+        unit = jnp.where(s * per_dev + j < HEADS + KV_HEADS, turned, unit)
+        heads_all[s, :, j * HEAD_DIM : (j + 1) * HEAD_DIM] = unit.astype(bf16)
+    copies = exchange(2, "seq", lambda peer: heads_all.at[s], heads_all.at[s])
+    started.extend(copies)
+    q_pairs[...] = jnp.zeros_like(q_pairs)
+    arrive(copies)
+
+    def head(h):
+        lane = (h % per_dev) * HEAD_DIM
+        return heads_all[h // per_dev, :, lane : lane + HEAD_DIM]
+
+    n_q = REQ_GRP * QROWS
+    spread_row = lax.broadcasted_iota(jnp.int32, (n_q, GROUP_Q * GROWS), 0)
+    spread_col = lax.broadcasted_iota(jnp.int32, (n_q, GROUP_Q * GROWS), 1)
+    spread = (
+        (spread_row // QROWS == spread_col % GROWS // STEPS)
+        & (spread_row % QROWS // STEPS == spread_col // GROWS)
+        & (spread_row % STEPS == spread_col % STEPS)
+    ).astype(f32).astype(bf16)
+    for k in range(KV_HEADS):
+        stacked = jnp.concatenate([head(k * GROUP_Q + j) for j in range(GROUP_Q)], axis=0)
+        placed = jnp.dot(spread, stacked, preferred_element_type=f32).astype(bf16)
+        for r in range(REQ_GRP):
+            q_pairs[
+                r,
+                k // 2,
+                (k % 2) * QROWS : (k % 2 + 1) * QROWS,
+                (k % 2) * HEAD_DIM : (k % 2 + 1) * HEAD_DIM,
+            ] = placed[r * QROWS : (r + 1) * QROWS]
+        new_k[:, k * HEAD_DIM : (k + 1) * HEAD_DIM] = head(HEADS + k)
+        new_v[:, k * HEAD_DIM : (k + 1) * HEAD_DIM] = head(HEADS + KV_HEADS + k)
+
+    loads[1].wait()
+    loads[2].wait()
+    score_scale = HEAD_DIM ** (-0.5)
+    new_row = lax.broadcasted_iota(jnp.int32, (2 * QROWS, GROWS), 0)
+    new_col = lax.broadcasted_iota(jnp.int32, (2 * QROWS, GROWS), 1)
+    causal = (new_col % STEPS <= new_row % STEPS) & (s == N_SEQ - 1)
+    columns = lax.broadcasted_iota(jnp.int32, (2 * QROWS, SHARD_ROWS), 1)
+    contract_last = (((1,), (1,)), ((), ()))
+
+    def attend(r, carry):
+        request = group_perm[g * REQ_GRP + r]
+        live = columns < lengths[request] - s * SHARD_ROWS
+        own = causal & (new_col // STEPS == r)
+        slots = [page_table[request, s * SHARD_PAGES + p] for p in range(SHARD_PAGES)]
+        for pair in range(KV_HEADS // 2):
+            lanes = slice(pair * 256, (pair + 1) * 256)
+            query = q_pairs[r, pair]
+            keys = jnp.concatenate([k_pool[slot, :, lanes] for slot in slots], axis=0)
+            values = jnp.concatenate([v_pool[slot, :, lanes] for slot in slots], axis=0)
+            scores = (
+                lax.dot_general(query, keys, contract_last, preferred_element_type=f32)
+                * score_scale
+            )
+            scores = jnp.where(live, scores, LOW_SCORE)
+            fresh = (
+                lax.dot_general(query, new_k[:, lanes], contract_last, preferred_element_type=f32)
+                * score_scale
+            )
+            fresh = jnp.where(own, fresh, LOW_SCORE)
+            top = jnp.maximum(
+                jnp.max(scores, axis=1, keepdims=True), jnp.max(fresh, axis=1, keepdims=True)
+            )
+            weights = jnp.where(live, jnp.exp(scores - top), 0.0)
+            new_weights = jnp.where(own, jnp.exp(fresh - top), 0.0)
+            total = jnp.sum(weights, axis=1, keepdims=True) + jnp.sum(
+                new_weights, axis=1, keepdims=True
+            )
+            weighted = jnp.dot(weights.astype(bf16), values, preferred_element_type=f32) + jnp.dot(
+                new_weights.astype(bf16), new_v[:, lanes], preferred_element_type=f32
+            )
+            block = stat_lanes(split_bf16(top, 3) + split_bf16(total, 2), 2 * QROWS)
+            rows = pl.ds(pl.multiple_of(r * QROWS, QROWS), QROWS)
+            for k in range(2):
+                mine = slice(k * QROWS, (k + 1) * QROWS)
+                att_send[2 * pair + k, rows, :HEAD_DIM] = weighted[
+                    mine, k * HEAD_DIM : (k + 1) * HEAD_DIM
+                ].astype(bf16)
+                att_send[2 * pair + k, rows, HEAD_DIM:] = block[mine].astype(bf16)
+        return carry
+
+    lax.fori_loop(0, REQ_GRP, attend, 0)
+    copies = exchange(3, "seq", lambda peer: att_send.at[peer], att_recv.at[s])
+    started.extend(copies)
+    att_recv[s] = att_send[s]
+    arrive(copies)
+
+    tops, sums = [], []
+    for i in range(N_SEQ):
+        block = att_recv[i, :, HEAD_DIM:].astype(f32)
+        tops.append(block[:, 0:1] + block[:, 1:2] + block[:, 2:3])
+        sums.append(block[:, 3:4] + block[:, 4:5])
+    best = functools.reduce(jnp.maximum, tops)
+    total = jnp.zeros((n_q, 1), f32)
+    weighted = jnp.zeros((n_q, HEAD_DIM), f32)
+    for i in range(N_SEQ):
+        factor = jnp.exp(tops[i] - best)
+        total = total + factor * sums[i]
+        weighted = weighted + factor * att_recv[i, :, :HEAD_DIM].astype(f32)
+    attended = (weighted / total).astype(bf16)
+    pick_row = lax.broadcasted_iota(jnp.int32, (GROUP_Q * GROWS, n_q), 0)
+    pick_col = lax.broadcasted_iota(jnp.int32, (GROUP_Q * GROWS, n_q), 1)
+    pick = (
+        (pick_col // QROWS == pick_row % GROWS // STEPS)
+        & (pick_col % QROWS // STEPS == pick_row // GROWS)
+        & (pick_col % STEPS == pick_row % STEPS)
+    ).astype(f32).astype(bf16)
+    picked = jnp.dot(pick, attended, preferred_element_type=f32).astype(bf16)
+    for j in range(GROUP_Q):
+        att_all[g, :, j * HEAD_DIM : (j + 1) * HEAD_DIM] = picked[j * GROWS : (j + 1) * GROWS]
+    copies = exchange(4, "grp", lambda peer: att_all.at[g], att_all.at[g])
+    started.extend(copies)
+    loads[3].wait()
+    arrive(copies)
+
+    def scatter_features(stage, send, recv):
+        for i in range(N_SEQ):
+            first = i * FEAT // 128 * 128
+            window = wide[:, first : first + 384]
+            if i * FEAT - first:
+                window = pltpu.roll(window, 384 - (i * FEAT - first), 1)
+            send[i] = window[:, :FEAT_PAD].astype(bf16)
+        copies = exchange(stage, "seq", lambda peer: send.at[peer], recv.at[s])
+        started.extend(copies)
+        recv[s] = send[s]
+        arrive(copies)
+        return sum(recv[i].astype(f32) for i in range(N_SEQ))
+
+    columns_in = jnp.concatenate([att_all[i] for i in range(N_GRP)], axis=0)
+    wide[:, DEPTH:] = jnp.zeros((ROWS, 128), f32)
+    wide[:, :DEPTH] = jnp.dot(columns_in, w_o[...], preferred_element_type=f32)
+    attn_sum = scatter_features(5, o_send, o_recv)
+    feature = lax.broadcasted_iota(jnp.int32, (ROWS, FEAT_PAD), 1) < FEAT
+    residual = jnp.where(feature, sorted_rows + attn_sum, 0.0)
+    mid_all[s] = feature_block(residual, gain_mid[...])
+    squares_mid = gather_features(6, mid_all)
+
+    stats = stat_lanes(split_bf16(squares_mid, 2), ROWS).astype(bf16)
+    for i in range(N_GRP):
+        ff_send[i, :, 3584:] = stats[i * GROWS : (i + 1) * GROWS]
+
+    for at, (weight, load) in enumerate([(w_gate, loads[4]), (w_up, loads[5])]):
+        load.wait()
+
+        def ff_tile(c, carry, at=at, weight=weight):
+            first = pl.multiple_of(c * 256, 256)
+            tile = jnp.dot(
+                x_bf[...], weight[:, pl.ds(first, 256)], preferred_element_type=f32
+            ).astype(bf16)
+            for i in range(N_GRP):
+                ff_send[i, :, pl.ds(pl.multiple_of(at * 1792 + first, 256), 256)] = tile[
+                    i * GROWS : (i + 1) * GROWS
+                ]
+            return carry
+
+        lax.fori_loop(0, 6, ff_tile, 0)
+        tile = jnp.dot(x_bf[...], weight[:, 1536:1728], preferred_element_type=f32)
+        tile = jnp.concatenate([tile, jnp.zeros((ROWS, 64), f32)], axis=1).astype(bf16)
+        for i in range(N_GRP):
+            ff_send[i, :, at * 1792 + 1536 : (at + 1) * 1792] = tile[i * GROWS : (i + 1) * GROWS]
+    copies = exchange(7, "grp", lambda peer: ff_send.at[peer], ff_recv.at[g])
+    started.extend(copies)
+    ff_recv[g] = ff_send[g]
+    arrive(copies)
+    stat = sum(ff_recv[i, :, 3584:].astype(f32) for i in range(N_GRP))
+    scale = lax.rsqrt(jnp.sum(stat, axis=1, keepdims=True) / D + EPSILON)
+    gate = sum(ff_recv[i, :, :1792].astype(f32) for i in range(N_GRP)) * scale
+    up = sum(ff_recv[i, :, 1792:3584].astype(f32) for i in range(N_GRP)) * scale
+    hid_all[g] = (gate / (1.0 + jnp.exp(-gate)) * up).astype(bf16)
+    copies = exchange(8, "grp", lambda peer: hid_all.at[g], hid_all.at[g])
+    started.extend(copies)
+    loads[6].wait()
+    arrive(copies)
+
+    def down_tile(c, carry):
+        first = pl.multiple_of(c * 256, 256)
+        hidden = jnp.concatenate([hid_all[i, :, :1728] for i in range(N_GRP)], axis=0)
+        wide[:, pl.ds(first, 256)] = jnp.dot(
+            hidden, w_down[:, pl.ds(first, 256)], preferred_element_type=f32
+        )
+        return carry
+
+    lax.fori_loop(0, DEPTH // 256, down_tile, 0)
+    down_sum = scatter_features(9, down_send, down_recv)
+    final = (residual + down_sum).astype(bf16)
+    origin = jnp.zeros((ROWS, ROWS), jnp.int32)
+    for i in range(ROWS // STEPS):
+        origin = jnp.where(col_i // STEPS == i, group_perm[i], origin)
+    back = (
+        ((row_i // STEPS) == origin) & ((col_i % STEPS) == (row_i % STEPS))
+    ).astype(f32).astype(bf16)
+    out[...] = jnp.dot(back, final, preferred_element_type=f32).astype(bf16)
+    for copy in started:
+        copy.wait_send()
+
+
+def fused_body(
+    tokens,
+    lengths,
+    group_perm,
+    page_table,
+    k_pool,
+    v_pool,
+    gain_in,
+    qkv_weight,
+    qkv_bias,
+    o_weight,
+    gain_mid,
+    gate_weight,
+    up_weight,
+    down_weight,
+):
+    pad = FEAT_PAD - FEAT
+    rows = jnp.pad(tokens.reshape(ROWS, FEAT), ((0, 0), (0, pad)))
+    gains = [jnp.pad(gain.reshape(1, FEAT), ((0, 0), (0, pad))) for gain in (gain_in, gain_mid)]
+    smem = pl.BlockSpec(memory_space=pltpu.SMEM)
+    vmem = pl.BlockSpec(memory_space=pltpu.VMEM)
+    hbm = pl.BlockSpec(memory_space=pl.ANY)
+    bf16, f32 = jnp.bfloat16, jnp.float32
+    out = pl.pallas_call(
+        fused_kernel,
+        out_shape=jax.ShapeDtypeStruct((ROWS, FEAT_PAD), bf16),
+        in_specs=[smem] * 3 + [vmem] * 4 + [hbm] * 7,
+        out_specs=vmem,
+        scratch_shapes=[
+            pltpu.VMEM(k_pool.shape, bf16),
+            pltpu.VMEM(v_pool.shape, bf16),
+            pltpu.VMEM(qkv_weight.shape, bf16),
+            pltpu.VMEM(o_weight.shape, bf16),
+            pltpu.VMEM(gate_weight.shape, bf16),
+            pltpu.VMEM(up_weight.shape, bf16),
+            pltpu.VMEM(down_weight.shape, bf16),
+            pltpu.VMEM((N_SEQ, ROWS, FEAT_PAD), bf16),
+            pltpu.VMEM((ROWS, DEPTH + 128), f32),
+            pltpu.VMEM((ROWS, DEPTH), bf16),
+            pltpu.VMEM((N_GRP, GROWS, 1024), bf16),
+            pltpu.VMEM((N_GRP, GROWS, 1024), bf16),
+            pltpu.VMEM((N_SEQ, GROWS, 896), bf16),
+            pltpu.VMEM((REQ_GRP, KV_HEADS // 2, 2 * QROWS, 256), bf16),
+            pltpu.VMEM((GROWS, KV_HEADS * HEAD_DIM), bf16),
+            pltpu.VMEM((GROWS, KV_HEADS * HEAD_DIM), bf16),
+            pltpu.VMEM((N_SEQ, REQ_GRP * QROWS, 2 * HEAD_DIM), bf16),
+            pltpu.VMEM((N_SEQ, REQ_GRP * QROWS, 2 * HEAD_DIM), bf16),
+            pltpu.VMEM((N_GRP, GROWS, GROUP_Q * HEAD_DIM), bf16),
+            pltpu.VMEM((ROWS, DEPTH + 128), f32),
+            pltpu.VMEM((N_SEQ, ROWS, FEAT_PAD), bf16),
+            pltpu.VMEM((N_SEQ, ROWS, FEAT_PAD), bf16),
+            pltpu.VMEM((N_SEQ, ROWS, FEAT_PAD), bf16),
+            pltpu.VMEM((N_GRP, GROWS, 3712), bf16),
+            pltpu.VMEM((N_GRP, GROWS, 3712), bf16),
+            pltpu.VMEM((N_GRP, GROWS, 1792), bf16),
+            pltpu.VMEM((N_SEQ, ROWS, FEAT_PAD), bf16),
+            pltpu.VMEM((N_SEQ, ROWS, FEAT_PAD), bf16),
+            pltpu.SemaphoreType.DMA((7,)),
+            pltpu.SemaphoreType.DMA((10, N_SEQ)),
+            pltpu.SemaphoreType.DMA((10, N_SEQ)),
+        ],
+        compiler_params=pltpu.CompilerParams(
+            collective_id=0, has_side_effects=True, vmem_limit_bytes=56 * 2**20
+        ),
+    )(
+        lengths,
+        group_perm,
+        page_table,
+        rows,
+        gains[0],
+        qkv_bias.reshape(1, -1),
+        gains[1],
+        k_pool,
+        v_pool,
+        qkv_weight,
+        o_weight,
+        gate_weight,
+        up_weight,
+        down_weight,
+    )
+    return out[:, :FEAT].reshape(tokens.shape)
+
+
 def solution(mesh):
+    fused = mesh.shape["seq"] == KV_HEADS and mesh.shape["grp"] == N_GRP
     return jax.shard_map(
-        body,
+        fused_body if fused else body,
         mesh=mesh,
         in_specs=(
             P(None, None, ("grp", "seq")),

time: 584 us -> 108 us (0.18)
  blocking collectives: 243 us -> 0 us
  waiting for transfers between devices: 228 us -> 0 us
  Pallas kernels: 0 us -> 85.2 us
  local copies, waits for them, and re-layouts: 47.4 us -> 20.9 us
  matrix products: 25.4 us -> 0 us
  other arithmetic: 23.7 us -> 0 us
  between operations: 14.8 us -> 0.01 us
    unnamed x8 -> x0, waiting for transfers between devices: 148 us -> none
    all_gather x4 -> x0, blocking collectives: 107 us -> none  [the longest x1 35.1 us: body(): lax.all_gather(normed_in, 'seq', axis=2, tiled=True)]
    psum x3 -> x0, blocking collectives: 99.6 us -> none  [the longest x1 42 us: body(): lax.psum(jnp.sum(sorted_rows * sorted_rows, axis=-1), ('grp', 'seq'))]
    pallas_call x0 -> x1, Pallas kernels: none -> 85.2 us  [fused_body(): pl.pallas_call(fused_kernel, out_shape=jax.ShapeDtypeStruct((ROWS, FEAT_P...]
    psum x2 -> x0, waiting for transfers between devices: 79.7 us -> none  [the longest x1 47.8 us: body(): lax.psum((weighted * factor[..., None]).astype(jnp.bfloat16), 'seq')]
    pmax x1 -> x0, blocking collectives: 37.1 us -> none  [body(): top_score = lax.pmax(best_score, 'seq')]
    gather x8 -> x0, local copies, waits for them, and re-layouts: 27.7 us -> none  [the longest x2 12.3 us: advance_all(): jnp.take(v_pool, slot_ids.reshape(-1), axis=0)]
    dot_general x11 -> x0, matrix products: 25.4 us -> none  [the longest x3 9.71 us: absorb(): jnp.einsum('hqd,khd->hqk', query_mat, key_block, preferred_element_type=j...]
  transfers between devices with their start and end apart: 5 -> 0, of which waited for: 5 -> 0; matrix products, arithmetic and copies ran while one was open for 1% -> 0% of each run, Pallas kernels for 0% -> 0%
where the time goes in v1:
time: 108 us; the launch traced here: 106 us
  Pallas kernels  85.2 us (79%)
  local copies, waits for them, and re-layouts  20.9 us (19%)
    pallas_call x1, Pallas kernels, fused_body(): pl.pallas_call(fused_kernel, out_shape=jax.ShapeDtypeStruct((ROWS, FEAT_P...  85.2 us
    unnamed x2, local copies, waits for them, and re-layouts  14.4 us
    pad x2, local copies, waits for them, and re-layouts, fused_body(): jnp.pad(gain.reshape(1, FEAT), ((0, 0), (0, pad)))  2.4 us

profile of v1, /device:TPU:0, one launch (start us, length us, event | category | flops | bytes accessed | tf_op | source)
XLA Modules:
  0.0 106.1 jit_solution(9997558150029277789)
XLA Ops:
  0.0 1.2 %pad.12.gain_in = f32[1,256]{1,0:T(1,128)} pad(f32[1,160]{1,0:T(1,128)} %bitcast.4, f32[]{:T(128)} %constant.4.clone.1), padding=0_0x0_96 | pad | bytes 1668 | tf_op jit(solution)/shard_map/jit(_pad)/pad | solution.py:624
  1.2 1.2 %pad.13.gain_mid = f32[1,256]{1,0:T(1,128)} pad(f32[1,160]{1,0:T(1,128)} %bitcast.5, f32[]{:T(128)} %constant.4.clone.1), padding=0_0x0_96 | pad | bytes 1668 | tf_op jit(solution)/shard_map/jit(_pad)/pad | solution.py:624
  2.4 1.3 %reshape.17.qkv_bias = f32[1,896]{1,0:T(1,128)} reshape(f32[896]{0:T(1024)} %param.22) | data formatting | bytes 7168 | tf_op jit(solution)/shard_map/reshape | solution.py:676
  3.7 0.8 reshape.15
  4.5 0.6 pad.11.tokens
  5.1 7.2 %copy.15.gate_hbm = bf16[1280,1728]{1,0:T(8,128)(2,1)} copy(bf16[1280,1728]{0,1:T(8,128)(2,1)} %param.25) | data formatting | bytes 8847360 | tf_op args[11]
  12.3 7.2 %copy.16.up_hbm = bf16[1280,1728]{1,0:T(8,128)(2,1)} copy(bf16[1280,1728]{0,1:T(8,128)(2,1)} %param.26) | data formatting | bytes 8847360 | tf_op args[12]
  19.5 85.2 %shard_map.136 = bf16[64,256]{1,0:T(8,128)(2,1)} custom-call(s32[16]{0:T(128)} %lengths.1, s32[16]{0:T(128)} %group_perm.1, s32[16,64]{1,0:T(8,128)} %page_table.1, bf16[64,256]{1,0:T(8,128)(2,1)} %pad.11.tokens, f32[1,256]{1,0:T(1,128)} %pad.12.gain_in, f32[1,896]{1,0:T(1,128)} %reshape.17.qkv_bias, f32[1,256]{1,0:T(1,128)} %pad.13.gain_mid, ...), custom_call_target="tpu_custom_call" | custom-call | tf_op jit(solution)/shard_map/pallas_call | solution.py:629
  104.7 1.4 %reshape.19 = bf16[16,4,160]{2,1,0:T(4,128)(2,1)} reshape(bf16[64,160]{1,0:T(8,128)(2,1)} %bitcast.3) | data formatting | bytes 40960 | tf_op jit(solution)/shard_map/reshape | solution.py:686

commit v2 on v1

--- a/solution.py
+++ b/solution.py
@@ -232,6 +232,26 @@
         pieces.append(piece)
         value = value - piece
     return pieces
+
+
+def pack(values, parts):
+    rows, width = ROWS // parts, 128 // parts
+    rest = values[:, 128:]
+    below = rest[:rows]
+    for a in range(1, parts):
+        below = below + pltpu.roll(rest[a * rows : (a + 1) * rows], a * width, 1)
+    return jnp.concatenate([values[:, :128], below], axis=0).astype(jnp.bfloat16)
+
+
+def unpack(block, parts):
+    rows, width = ROWS // parts, 128 // parts
+    below = block[ROWS:]
+    lane = lax.broadcasted_iota(jnp.int32, (rows, 128), 1)
+    rest = [
+        jnp.where(lane < width, pltpu.roll(below, 128 - a * width, 1) if a else below, 0.0)
+        for a in range(parts)
+    ]
+    return jnp.concatenate([block[:ROWS], jnp.concatenate(rest, axis=0)], axis=1)
 
 
 def fused_kernel(
@@ -266,6 +286,7 @@
     q_pairs,
     new_k,
     new_v,
+    att_held,
     att_send,
     att_recv,
     att_all,
@@ -273,11 +294,15 @@
     o_send,
     o_recv,
     mid_all,
-    ff_send,
-    ff_recv,
+    gate_send,
+    gate_recv,
+    up_send,
+    up_recv,
     hid_all,
     down_send,
     down_recv,
+    padded,
+    gains,
     load_sem,
     send_sem,
     recv_sem,
@@ -335,23 +360,21 @@
 
     started = []
 
-    row_i = lax.broadcasted_iota(jnp.int32, (ROWS, ROWS), 0)
-    col_i = lax.broadcasted_iota(jnp.int32, (ROWS, ROWS), 1)
-    origin = jnp.zeros((ROWS, ROWS), jnp.int32)
+    padded[...] = jnp.zeros_like(padded)
     for i in range(ROWS // STEPS):
-        origin = jnp.where(row_i // STEPS == i, group_perm[i], origin)
-    order = (
-        ((col_i // STEPS) == origin) & ((col_i % STEPS) == (row_i % STEPS))
-    ).astype(f32).astype(bf16)
-    sorted_rows = jnp.dot(order, tokens[...], preferred_element_type=f32)
+        padded[i * STEPS : (i + 1) * STEPS, :FEAT] = tokens[group_perm[i]].astype(f32)
+    gains[...] = jnp.zeros_like(gains)
+    gains[0:1, :FEAT] = gain_in[...]
+    gains[1:2, :FEAT] = gain_mid[...]
+    sorted_rows = padded[...]
 
     def feature_block(values, gain):
         squares = jnp.sum(values * values, axis=1, keepdims=True)
-        return stat_lanes(
-            split_bf16(squares, 2), ROWS, FEAT, FEAT_PAD, values * gain
-        ).astype(bf16)
-
-    x_all[s] = feature_block(sorted_rows, gain_in[...])
+        return pack(
+            stat_lanes(split_bf16(squares, 2), ROWS, FEAT, FEAT_PAD, values * gain), 2
+        )
+
+    x_all[s] = feature_block(sorted_rows, gains[0:1, :])
     pl.semaphore_wait(barrier, N_SEQ + N_GRP - 2)
 
     def gather_features(stage, blocks):
@@ -362,7 +385,7 @@
         x_wide[...] = jnp.zeros_like(x_wide)
         squares = jnp.zeros((ROWS, 1), f32)
         for i in range(N_SEQ):
-            block = blocks[i].astype(f32)
+            block = unpack(blocks[i].astype(f32), 2)
             kept = jnp.where(lane < FEAT, block, 0.0)
             squares = squares + jnp.sum(block - kept, axis=1, keepdims=True)
             first = i * FEAT // 128 * 128
@@ -401,7 +424,7 @@
     arrive(copies)
     summed = sum(qkv_recv[i].astype(f32) for i in range(N_GRP))
     scale = lax.rsqrt(jnp.sum(summed[:, 896:], axis=1, keepdims=True) / D + EPSILON)
-    share = summed[:, :896] * scale + qkv_bias[...]
+    share = summed[:, :896] * scale + qkv_bias[...].reshape(1, 896)
     per_dev = 896 // HEAD_DIM
     for j in range(per_dev):
         unit = share[:, j * HEAD_DIM : (j + 1) * HEAD_DIM]
@@ -482,31 +505,13 @@
             rows = pl.ds(pl.multiple_of(r * QROWS, QROWS), QROWS)
             for k in range(2):
                 mine = slice(k * QROWS, (k + 1) * QROWS)
-                att_send[2 * pair + k, rows, :HEAD_DIM] = weighted[
+                att_held[2 * pair + k, rows, :HEAD_DIM] = weighted[
                     mine, k * HEAD_DIM : (k + 1) * HEAD_DIM
                 ].astype(bf16)
-                att_send[2 * pair + k, rows, HEAD_DIM:] = block[mine].astype(bf16)
+                att_held[2 * pair + k, rows, HEAD_DIM:] = block[mine].astype(bf16)
         return carry
 
     lax.fori_loop(0, REQ_GRP, attend, 0)
-    copies = exchange(3, "seq", lambda peer: att_send.at[peer], att_recv.at[s])
-    started.extend(copies)
-    att_recv[s] = att_send[s]
-    arrive(copies)
-
-    tops, sums = [], []
-    for i in range(N_SEQ):
-        block = att_recv[i, :, HEAD_DIM:].astype(f32)
-        tops.append(block[:, 0:1] + block[:, 1:2] + block[:, 2:3])
-        sums.append(block[:, 3:4] + block[:, 4:5])
-    best = functools.reduce(jnp.maximum, tops)
-    total = jnp.zeros((n_q, 1), f32)
-    weighted = jnp.zeros((n_q, HEAD_DIM), f32)
-    for i in range(N_SEQ):
-        factor = jnp.exp(tops[i] - best)
-        total = total + factor * sums[i]
-        weighted = weighted + factor * att_recv[i, :, :HEAD_DIM].astype(f32)
-    attended = (weighted / total).astype(bf16)
     pick_row = lax.broadcasted_iota(jnp.int32, (GROUP_Q * GROWS, n_q), 0)
     pick_col = lax.broadcasted_iota(jnp.int32, (GROUP_Q * GROWS, n_q), 1)
     pick = (
@@ -514,13 +519,43 @@
         & (pick_col % QROWS // STEPS == pick_row // GROWS)
         & (pick_col % STEPS == pick_row % STEPS)
     ).astype(f32).astype(bf16)
-    picked = jnp.dot(pick, attended, preferred_element_type=f32).astype(bf16)
+    n_out = GROUP_Q * GROWS
+    for k in range(KV_HEADS):
+        picked = jnp.dot(pick, att_held[k], preferred_element_type=f32)
+        below = picked[:GROWS, HEAD_DIM:]
+        for j in range(1, GROUP_Q):
+            below = below + pltpu.roll(picked[j * GROWS : (j + 1) * GROWS, HEAD_DIM:], 8 * j, 1)
+        att_send[k, :n_out] = picked[:, :HEAD_DIM].astype(bf16)
+        att_send[k, n_out:] = below.astype(bf16)
+    copies = exchange(3, "seq", lambda peer: att_send.at[peer], att_recv.at[s])
+    started.extend(copies)
+    att_recv[s] = att_send[s]
+    arrive(copies)
+
+    stat_lane = lax.broadcasted_iota(jnp.int32, (GROWS, HEAD_DIM), 1) % 8 == 0
+    tops, sums = [], []
+    for i in range(N_SEQ):
+        block = att_recv[i, n_out:, :].astype(f32)
+        shifted = [block] + [pltpu.roll(block, HEAD_DIM - n, 1) for n in range(1, 5)]
+        tops.append(jnp.where(stat_lane, shifted[0] + shifted[1] + shifted[2], 0.0))
+        sums.append(jnp.where(stat_lane, shifted[3] + shifted[4], 1.0))
+    best = functools.reduce(jnp.maximum, tops)
+    factors = [jnp.exp(top - best) for top in tops]
+    total = sum(factor * part_sum for factor, part_sum in zip(factors, sums))
     for j in range(GROUP_Q):
-        att_all[g, :, j * HEAD_DIM : (j + 1) * HEAD_DIM] = picked[j * GROWS : (j + 1) * GROWS]
+        rows = slice(j * GROWS, (j + 1) * GROWS)
+        weighted = sum(
+            factors[i][:, 8 * j : 8 * j + 1] * att_recv[i, rows, :].astype(f32)
+            for i in range(N_SEQ)
+        )
+        attended = weighted / total[:, 8 * j : 8 * j + 1]
+        att_all[g, :, j * HEAD_DIM : (j + 1) * HEAD_DIM] = attended.astype(bf16)
     copies = exchange(4, "grp", lambda peer: att_all.at[g], att_all.at[g])
     started.extend(copies)
     loads[3].wait()
     arrive(copies)
+
+    feature = lax.broadcasted_iota(jnp.int32, (ROWS, FEAT_PAD), 1) < FEAT
 
     def scatter_features(stage, send, recv):
         for i in range(N_SEQ):
@@ -528,54 +563,61 @@
             window = wide[:, first : first + 384]
             if i * FEAT - first:
                 window = pltpu.roll(window, 384 - (i * FEAT - first), 1)
-            send[i] = window[:, :FEAT_PAD].astype(bf16)
+            send[i] = pack(jnp.where(feature, window[:, :FEAT_PAD], 0.0), 4)
         copies = exchange(stage, "seq", lambda peer: send.at[peer], recv.at[s])
         started.extend(copies)
         recv[s] = send[s]
         arrive(copies)
-        return sum(recv[i].astype(f32) for i in range(N_SEQ))
+        return unpack(sum(recv[i].astype(f32) for i in range(N_SEQ)), 4)
 
     columns_in = jnp.concatenate([att_all[i] for i in range(N_GRP)], axis=0)
     wide[:, DEPTH:] = jnp.zeros((ROWS, 128), f32)
     wide[:, :DEPTH] = jnp.dot(columns_in, w_o[...], preferred_element_type=f32)
     attn_sum = scatter_features(5, o_send, o_recv)
-    feature = lax.broadcasted_iota(jnp.int32, (ROWS, FEAT_PAD), 1) < FEAT
-    residual = jnp.where(feature, sorted_rows + attn_sum, 0.0)
-    mid_all[s] = feature_block(residual, gain_mid[...])
+    residual = sorted_rows + attn_sum
+    mid_all[s] = feature_block(residual, gains[1:2, :])
     squares_mid = gather_features(6, mid_all)
 
     stats = stat_lanes(split_bf16(squares_mid, 2), ROWS).astype(bf16)
     for i in range(N_GRP):
-        ff_send[i, :, 3584:] = stats[i * GROWS : (i + 1) * GROWS]
-
-    for at, (weight, load) in enumerate([(w_gate, loads[4]), (w_up, loads[5])]):
-        load.wait()
-
-        def ff_tile(c, carry, at=at, weight=weight):
+        gate_send[i, :, 1792:] = stats[i * GROWS : (i + 1) * GROWS]
+
+    def project(weight, send):
+        def ff_tile(c, carry):
             first = pl.multiple_of(c * 256, 256)
-            tile = jnp.dot(
-                x_bf[...], weight[:, pl.ds(first, 256)], preferred_element_type=f32
+            tile = lax.dot_general(
+                x_bf[...], weight[pl.ds(first, 256), :], contract_last, preferred_element_type=f32
             ).astype(bf16)
             for i in range(N_GRP):
-                ff_send[i, :, pl.ds(pl.multiple_of(at * 1792 + first, 256), 256)] = tile[
-                    i * GROWS : (i + 1) * GROWS
-                ]
+                send[i, :, pl.ds(first, 256)] = tile[i * GROWS : (i + 1) * GROWS]
             return carry
 
         lax.fori_loop(0, 6, ff_tile, 0)
-        tile = jnp.dot(x_bf[...], weight[:, 1536:1728], preferred_element_type=f32)
+        tile = lax.dot_general(
+            x_bf[...], weight[1536:1728, :], contract_last, preferred_element_type=f32
+        )
         tile = jnp.concatenate([tile, jnp.zeros((ROWS, 64), f32)], axis=1).astype(bf16)
         for i in range(N_GRP):
-            ff_send[i, :, at * 1792 + 1536 : (at + 1) * 1792] = tile[i * GROWS : (i + 1) * GROWS]
-    copies = exchange(7, "grp", lambda peer: ff_send.at[peer], ff_recv.at[g])
-    started.extend(copies)
-    ff_recv[g] = ff_send[g]
-    arrive(copies)
-    stat = sum(ff_recv[i, :, 3584:].astype(f32) for i in range(N_GRP))
+            send[i, :, 1536:1792] = tile[i * GROWS : (i + 1) * GROWS]
+
+    loads[4].wait()
+    project(w_gate, gate_send)
+    gate_copies = exchange(7, "grp", lambda peer: gate_send.at[peer], gate_recv.at[g])
+    started.extend(gate_copies)
+    loads[5].wait()
+    project(w_up, up_send)
+    up_copies = exchange(10, "grp", lambda peer: up_send.at[peer], up_recv.at[g])
+    started.extend(up_copies)
+    gate_recv[g] = gate_send[g]
+    up_recv[g] = up_send[g]
+    arrive(gate_copies)
+    stat = sum(gate_recv[i, :, 1792:].astype(f32) for i in range(N_GRP))
     scale = lax.rsqrt(jnp.sum(stat, axis=1, keepdims=True) / D + EPSILON)
-    gate = sum(ff_recv[i, :, :1792].astype(f32) for i in range(N_GRP)) * scale
-    up = sum(ff_recv[i, :, 1792:3584].astype(f32) for i in range(N_GRP)) * scale
-    hid_all[g] = (gate / (1.0 + jnp.exp(-gate)) * up).astype(bf16)
+    gate = sum(gate_recv[i, :, :1792].astype(f32) for i in range(N_GRP)) * scale
+    gate = gate / (1.0 + jnp.exp(-gate))
+    arrive(up_copies)
+    up = sum(up_recv[i].astype(f32) for i in range(N_GRP)) * scale
+    hid_all[g] = (gate * up).astype(bf16)
     copies = exchange(8, "grp", lambda peer: hid_all.at[g], hid_all.at[g])
     started.extend(copies)
     loads[6].wait()
@@ -592,13 +634,17 @@
     lax.fori_loop(0, DEPTH // 256, down_tile, 0)
     down_sum = scatter_features(9, down_send, down_recv)
     final = (residual + down_sum).astype(bf16)
+    row_i = lax.broadcasted_iota(jnp.int32, (ROWS, ROWS), 0)
+    col_i = lax.broadcasted_iota(jnp.int32, (ROWS, ROWS), 1)
     origin = jnp.zeros((ROWS, ROWS), jnp.int32)
     for i in range(ROWS // STEPS):
         origin = jnp.where(col_i // STEPS == i, group_perm[i], origin)
     back = (
         ((row_i // STEPS) == origin) & ((col_i % STEPS) == (row_i % STEPS))
     ).astype(f32).astype(bf16)
-    out[...] = jnp.dot(back, final, preferred_element_type=f32).astype(bf16)
+    ordered = jnp.dot(back, final, preferred_element_type=f32)
+    for i in range(ROWS // STEPS):
+        out[i] = ordered[i * STEPS : (i + 1) * STEPS, :FEAT].astype(bf16)
     for copy in started:
         copy.wait_send()
 
@@ -619,16 +665,15 @@
     up_weight,
     down_weight,
 ):
-    pad = FEAT_PAD - FEAT
-    rows = jnp.pad(tokens.reshape(ROWS, FEAT), ((0, 0), (0, pad)))
-    gains = [jnp.pad(gain.reshape(1, FEAT), ((0, 0), (0, pad))) for gain in (gain_in, gain_mid)]
+    gains = [gain.reshape(1, FEAT) for gain in (gain_in, gain_mid)]
+    gate_rows, up_rows = gate_weight.T, up_weight.T
     smem = pl.BlockSpec(memory_space=pltpu.SMEM)
     vmem = pl.BlockSpec(memory_space=pltpu.VMEM)
     hbm = pl.BlockSpec(memory_space=pl.ANY)
     bf16, f32 = jnp.bfloat16, jnp.float32
-    out = pl.pallas_call(
+    return pl.pallas_call(
         fused_kernel,
-        out_shape=jax.ShapeDtypeStruct((ROWS, FEAT_PAD), bf16),
+        out_shape=jax.ShapeDtypeStruct(tokens.shape, bf16),
         in_specs=[smem] * 3 + [vmem] * 4 + [hbm] * 7,
         out_specs=vmem,
         scratch_shapes=[
@@ -636,10 +681,10 @@
             pltpu.VMEM(v_pool.shape, bf16),
             pltpu.VMEM(qkv_weight.shape, bf16),
             pltpu.VMEM(o_weight.shape, bf16),
-            pltpu.VMEM(gate_weight.shape, bf16),
-            pltpu.VMEM(up_weight.shape, bf16),
+            pltpu.VMEM(gate_rows.shape, bf16),
+            pltpu.VMEM(up_rows.shape, bf16),
             pltpu.VMEM(down_weight.shape, bf16),
-            pltpu.VMEM((N_SEQ, ROWS, FEAT_PAD), bf16),
+            pltpu.VMEM((N_SEQ, 96, 128), bf16),
             pltpu.VMEM((ROWS, DEPTH + 128), f32),
             pltpu.VMEM((ROWS, DEPTH), bf16),
             pltpu.VMEM((N_GRP, GROWS, 1024), bf16),
@@ -649,20 +694,25 @@
             pltpu.VMEM((GROWS, KV_HEADS * HEAD_DIM), bf16),
             pltpu.VMEM((GROWS, KV_HEADS * HEAD_DIM), bf16),
             pltpu.VMEM((N_SEQ, REQ_GRP * QROWS, 2 * HEAD_DIM), bf16),
-            pltpu.VMEM((N_SEQ, REQ_GRP * QROWS, 2 * HEAD_DIM), bf16),
+            pltpu.VMEM((N_SEQ, 96, 128), bf16),
+            pltpu.VMEM((N_SEQ, 96, 128), bf16),
             pltpu.VMEM((N_GRP, GROWS, GROUP_Q * HEAD_DIM), bf16),
             pltpu.VMEM((ROWS, DEPTH + 128), f32),
-            pltpu.VMEM((N_SEQ, ROWS, FEAT_PAD), bf16),
-            pltpu.VMEM((N_SEQ, ROWS, FEAT_PAD), bf16),
-            pltpu.VMEM((N_SEQ, ROWS, FEAT_PAD), bf16),
-            pltpu.VMEM((N_GRP, GROWS, 3712), bf16),
-            pltpu.VMEM((N_GRP, GROWS, 3712), bf16),
+            pltpu.VMEM((N_SEQ, 80, 128), bf16),
+            pltpu.VMEM((N_SEQ, 80, 128), bf16),
+            pltpu.VMEM((N_SEQ, 96, 128), bf16),
+            pltpu.VMEM((N_GRP, GROWS, 1920), bf16),
+            pltpu.VMEM((N_GRP, GROWS, 1920), bf16),
             pltpu.VMEM((N_GRP, GROWS, 1792), bf16),
-            pltpu.VMEM((N_SEQ, ROWS, FEAT_PAD), bf16),
-            pltpu.VMEM((N_SEQ, ROWS, FEAT_PAD), bf16),
+            pltpu.VMEM((N_GRP, GROWS, 1792), bf16),
+            pltpu.VMEM((N_GRP, GROWS, 1792), bf16),
+            pltpu.VMEM((N_SEQ, 80, 128), bf16),
+            pltpu.VMEM((N_SEQ, 80, 128), bf16),
+            pltpu.VMEM((ROWS, FEAT_PAD), f32),
+            pltpu.VMEM((8, FEAT_PAD), f32),
             pltpu.SemaphoreType.DMA((7,)),
-            pltpu.SemaphoreType.DMA((10, N_SEQ)),
-            pltpu.SemaphoreType.DMA((10, N_SEQ)),
+            pltpu.SemaphoreType.DMA((11, N_SEQ)),
+            pltpu.SemaphoreType.DMA((11, N_SEQ)),
         ],
         compiler_params=pltpu.CompilerParams(
             collective_id=0, has_side_effects=True, vmem_limit_bytes=56 * 2**20
@@ -671,19 +721,18 @@
         lengths,
         group_perm,
         page_table,
-        rows,
+        tokens,
         gains[0],
-        qkv_bias.reshape(1, -1),
+        qkv_bias,
         gains[1],
         k_pool,
         v_pool,
         qkv_weight,
         o_weight,
-        gate_weight,
-        up_weight,
+        gate_rows,
+        up_rows,
         down_weight,
     )
-    return out[:, :FEAT].reshape(tokens.shape)
 
 
 def solution(mesh):

time: 108 us -> 76.3 us (0.71); the launches traced: 106 us -> 76.1 us
  local copies, waits for them, and re-layouts: 20.9 us -> 1.39 us
  Pallas kernels: 85.2 us -> 74.7 us
    unnamed x2 -> x1, local copies, waits for them, and re-layouts: 14.4 us -> 1.39 us
    pallas_call x1, Pallas kernels: 85.2 us -> 74.7 us  [fused_body(): pl.pallas_call(fused_kernel, out_shape=jax.ShapeDtypeStruct(tokens.shape,...]
    reshape x3 -> x0, local copies, waits for them, and re-layouts: 3.45 us -> none  [the longest x1 1.39 us: fused_body(): return out[:, :FEAT].reshape(tokens.shape)]
    pad x3 -> x0, local copies, waits for them, and re-layouts: 3.02 us -> none  [the longest x2 2.4 us: fused_body(): jnp.pad(gain.reshape(1, FEAT), ((0, 0), (0, pad)))]
where the time goes in v2:
time: 76.3 us; the launch traced here: 76.1 us
  Pallas kernels  74.7 us (98%)
  local copies, waits for them, and re-layouts  1.39 us (2%)
    pallas_call x1, Pallas kernels, fused_body(): pl.pallas_call(fused_kernel, out_shape=jax.ShapeDtypeStruct(tokens.shape,...  74.7 us

profile of v2, /device:TPU:0, one launch (start us, length us, event | category | flops | bytes accessed | tf_op | source)
XLA Modules:
  0.0 76.1 jit_solution(1680103640502485271)
XLA Ops:
  0.0 74.7 %shard_map.136 = bf16[16,4,160]{2,1,0:T(4,128)(2,1)} custom-call(s32[16]{0:T(128)} %lengths.1, s32[16]{0:T(128)} %group_perm.1, s32[16,64]{1,0:T(8,128)} %page_table.1, bf16[16,4,160]{2,1,0:T(4,128)(2,1)} %tokens.1, f32[1,160]{1,0:T(1,128)} %bitcast.6, f32[896]{0:T(1024)} %qkv_bias.1, f32[1,160]{1,0:T(1,128)} %bitcast.7, bf16[32,128,1024]{2,1,0:T(8,128)(2,1)} %k_hbm.1, ...), custom_call_target="tpu_custom_call" | custom-call | tf_op jit(solution)/shard_map/pallas_call | solution.py:674
  74.7 1.4 %copy.16 = bf16[16,4,160]{2,1,0:T(4,128)(2,1)} copy(bf16[16,4,160]{2,1,0:T(4,128)(2,1)} %shard_map.136) | data formatting | bytes 40960

commit v3 on v2

--- a/solution.py
+++ b/solution.py
@@ -340,7 +340,7 @@
     def exchange(stage, axis, source, target):
         me, count = (s, N_SEQ) if axis == "seq" else (g, N_GRP)
         copies = []
-        for d in range(1, count):
+        for d in sorted(range(1, count), key=lambda d: abs(2 * d - count)):
             peer = lax.rem(me + d, count)
             copy = pltpu.make_async_remote_copy(
                 src_ref=source(peer),
@@ -354,6 +354,29 @@
             copies.append(copy)
         return copies
 
+    def gather_seq(stage, blocks):
+        partner = s + 1 - 2 * lax.rem(s, 2)
+
+        def push(block, peer, at):
+            copy = pltpu.make_async_remote_copy(
+                src_ref=blocks.at[block],
+                dst_ref=blocks.at[block],
+                send_sem=send_sem.at[stage, at],
+                recv_sem=recv_sem.at[stage, at],
+                device_id={"seq": peer},
+                device_id_type=MESH,
+            )
+            copy.start()
+            started.append(copy)
+            return copy
+
+        along = {d: push(s, lax.rem(s + d, N_SEQ), d) for d in (4, 2, 6)}
+        across = [push(s, partner, 1)]
+        for d in (2, 6, 4):
+            along[d].wait_recv()
+            across.append(push(lax.rem(s - d + N_SEQ, N_SEQ), partner, d + 1))
+        arrive(across)
+
     def arrive(copies):
         for copy in copies:
             copy.wait_recv()
@@ -361,6 +384,7 @@
     started = []
 
     padded[...] = jnp.zeros_like(padded)
+    wide[...] = jnp.zeros_like(wide)
     for i in range(ROWS // STEPS):
         padded[i * STEPS : (i + 1) * STEPS, :FEAT] = tokens[group_perm[i]].astype(f32)
     gains[...] = jnp.zeros_like(gains)
@@ -378,9 +402,7 @@
     pl.semaphore_wait(barrier, N_SEQ + N_GRP - 2)
 
     def gather_features(stage, blocks):
-        copies = exchange(stage, "seq", lambda peer: blocks.at[s], blocks.at[s])
-        started.extend(copies)
-        arrive(copies)
+        gather_seq(stage, blocks)
         lane = lax.broadcasted_iota(jnp.int32, (ROWS, FEAT_PAD), 1)
         x_wide[...] = jnp.zeros_like(x_wide)
         squares = jnp.zeros((ROWS, 1), f32)
@@ -431,10 +453,8 @@
         turned = unit * cosine + pltpu.roll(unit, half, 1) * sine
         unit = jnp.where(s * per_dev + j < HEADS + KV_HEADS, turned, unit)
         heads_all[s, :, j * HEAD_DIM : (j + 1) * HEAD_DIM] = unit.astype(bf16)
-    copies = exchange(2, "seq", lambda peer: heads_all.at[s], heads_all.at[s])
-    started.extend(copies)
     q_pairs[...] = jnp.zeros_like(q_pairs)
-    arrive(copies)
+    gather_seq(2, heads_all)
 
     def head(h):
         lane = (h % per_dev) * HEAD_DIM
@@ -511,44 +531,58 @@
                 att_held[2 * pair + k, rows, HEAD_DIM:] = block[mine].astype(bf16)
         return carry
 
-    lax.fori_loop(0, REQ_GRP, attend, 0)
-    pick_row = lax.broadcasted_iota(jnp.int32, (GROUP_Q * GROWS, n_q), 0)
-    pick_col = lax.broadcasted_iota(jnp.int32, (GROUP_Q * GROWS, n_q), 1)
+    half_rows = GROWS // 2
+    n_out = GROUP_Q * half_rows
+    pick_row = lax.broadcasted_iota(jnp.int32, (n_out, n_q // 2), 0)
+    pick_col = lax.broadcasted_iota(jnp.int32, (n_out, n_q // 2), 1)
     pick = (
-        (pick_col // QROWS == pick_row % GROWS // STEPS)
-        & (pick_col % QROWS // STEPS == pick_row // GROWS)
+        (pick_col // QROWS == pick_row % half_rows // STEPS)
+        & (pick_col % QROWS // STEPS == pick_row // half_rows)
         & (pick_col % STEPS == pick_row % STEPS)
     ).astype(f32).astype(bf16)
-    n_out = GROUP_Q * GROWS
-    for k in range(KV_HEADS):
-        picked = jnp.dot(pick, att_held[k], preferred_element_type=f32)
-        below = picked[:GROWS, HEAD_DIM:]
-        for j in range(1, GROUP_Q):
-            below = below + pltpu.roll(picked[j * GROWS : (j + 1) * GROWS, HEAD_DIM:], 8 * j, 1)
-        att_send[k, :n_out] = picked[:, :HEAD_DIM].astype(bf16)
-        att_send[k, n_out:] = below.astype(bf16)
-    copies = exchange(3, "seq", lambda peer: att_send.at[peer], att_recv.at[s])
-    started.extend(copies)
-    att_recv[s] = att_send[s]
-    arrive(copies)
-
-    stat_lane = lax.broadcasted_iota(jnp.int32, (GROWS, HEAD_DIM), 1) % 8 == 0
-    tops, sums = [], []
-    for i in range(N_SEQ):
-        block = att_recv[i, n_out:, :].astype(f32)
-        shifted = [block] + [pltpu.roll(block, HEAD_DIM - n, 1) for n in range(1, 5)]
-        tops.append(jnp.where(stat_lane, shifted[0] + shifted[1] + shifted[2], 0.0))
-        sums.append(jnp.where(stat_lane, shifted[3] + shifted[4], 1.0))
-    best = functools.reduce(jnp.maximum, tops)
-    factors = [jnp.exp(top - best) for top in tops]
-    total = sum(factor * part_sum for factor, part_sum in zip(factors, sums))
+    att_copies = []
+    for part in range(2):
+        lax.fori_loop(2 * part, 2 * part + 2, attend, 0)
+        for k in range(KV_HEADS):
+            held = att_held[k, part * n_q // 2 : (part + 1) * n_q // 2, :]
+            picked = jnp.dot(pick, held, preferred_element_type=f32)
+            below = picked[:half_rows, HEAD_DIM:]
+            for j in range(1, GROUP_Q):
+                stat = picked[j * half_rows : (j + 1) * half_rows, HEAD_DIM:]
+                below = below + pltpu.roll(stat, 8 * j, 1)
+            att_send[part, k] = jnp.concatenate([picked[:, :HEAD_DIM], below], axis=0).astype(bf16)
+        copies = exchange(
+            (3, 11)[part], "seq", lambda peer: att_send.at[part, peer], att_recv.at[part, s]
+        )
+        started.extend(copies)
+        att_copies.append(copies)
+        att_recv[part, s] = att_send[part, s]
+
+    stat_lane = lax.broadcasted_iota(jnp.int32, (half_rows, HEAD_DIM), 1) % 8 == 0
+    halves = []
+    for part in range(2):
+        arrive(att_copies[part])
+        blocks = [att_recv[part, i].astype(f32) for i in range(N_SEQ)]
+        tops, sums = [], []
+        for block in blocks:
+            below = block[n_out:]
+            shifted = [below] + [pltpu.roll(below, HEAD_DIM - n, 1) for n in range(1, 5)]
+            tops.append(jnp.where(stat_lane, shifted[0] + shifted[1] + shifted[2], 0.0))
+            sums.append(jnp.where(stat_lane, shifted[3] + shifted[4], 1.0))
+        best = functools.reduce(jnp.maximum, tops)
+        factors = [jnp.exp(top - best) for top in tops]
+        total = sum(factor * part_sum for factor, part_sum in zip(factors, sums))
+        joined = []
+        for j in range(GROUP_Q):
+            rows = slice(j * half_rows, (j + 1) * half_rows)
+            weighted = sum(
+                factor[:, 8 * j : 8 * j + 1] * block[rows]
+                for factor, block in zip(factors, blocks)
+            )
+            joined.append(weighted / total[:, 8 * j : 8 * j + 1])
+        halves.append(joined)
     for j in range(GROUP_Q):
-        rows = slice(j * GROWS, (j + 1) * GROWS)
-        weighted = sum(
-            factors[i][:, 8 * j : 8 * j + 1] * att_recv[i, rows, :].astype(f32)
-            for i in range(N_SEQ)
-        )
-        attended = weighted / total[:, 8 * j : 8 * j + 1]
+        attended = jnp.concatenate([halves[0][j], halves[1][j]], axis=0)
         att_all[g, :, j * HEAD_DIM : (j + 1) * HEAD_DIM] = attended.astype(bf16)
     copies = exchange(4, "grp", lambda peer: att_all.at[g], att_all.at[g])
     started.extend(copies)
@@ -557,23 +591,49 @@
 
     feature = lax.broadcasted_iota(jnp.int32, (ROWS, FEAT_PAD), 1) < FEAT
 
-    def scatter_features(stage, send, recv):
+    def scatter_features(stage, rows, weight, send, recv):
+        def copy_of(i, source):
+            return pltpu.make_async_remote_copy(
+                src_ref=send.at[i],
+                dst_ref=recv.at[source],
+                send_sem=send_sem.at[stage, i],
+                recv_sem=recv_sem.at[stage, source],
+                device_id={"seq": i},
+                device_id_type=MESH,
+            )
+
+        parts = [
+            (((0, 384), (896, DEPTH)), (0, 7, 1, 6)),
+            (((384, 896),), (2, 5, 3, 4)),
+        ]
+        for pieces, peers in parts:
+            for begin, end in pieces:
+                wide[:, begin:end] = jnp.dot(
+                    rows, weight[:, begin:end], preferred_element_type=f32
+                )
+            for i in peers:
+                first = i * FEAT // 128 * 128
+                window = wide[:, first : first + 384]
+                if i * FEAT - first:
+                    window = pltpu.roll(window, 384 - (i * FEAT - first), 1)
+                send[i] = pack(jnp.where(feature, window[:, :FEAT_PAD], 0.0), 4)
+
+                @pl.when(s != i)
+                def _(i=i):
+                    copy_of(i, s).start()
+
+        recv[s] = send[s]
         for i in range(N_SEQ):
-            first = i * FEAT // 128 * 128
-            window = wide[:, first : first + 384]
-            if i * FEAT - first:
-                window = pltpu.roll(window, 384 - (i * FEAT - first), 1)
-            send[i] = pack(jnp.where(feature, window[:, :FEAT_PAD], 0.0), 4)
-        copies = exchange(stage, "seq", lambda peer: send.at[peer], recv.at[s])
-        started.extend(copies)
-        recv[s] = send[s]
-        arrive(copies)
+
+            @pl.when(s != i)
+            def _(i=i):
+                copy_of(i, i).wait_recv()
+                copy_of(i, i).wait_send()
+
         return unpack(sum(recv[i].astype(f32) for i in range(N_SEQ)), 4)
 
     columns_in = jnp.concatenate([att_all[i] for i in range(N_GRP)], axis=0)
-    wide[:, DEPTH:] = jnp.zeros((ROWS, 128), f32)
-    wide[:, :DEPTH] = jnp.dot(columns_in, w_o[...], preferred_element_type=f32)
-    attn_sum = scatter_features(5, o_send, o_recv)
+    attn_sum = scatter_features(5, columns_in, w_o, o_send, o_recv)
     residual = sorted_rows + attn_sum
     mid_all[s] = feature_block(residual, gains[1:2, :])
     squares_mid = gather_features(6, mid_all)
@@ -623,16 +683,8 @@
     loads[6].wait()
     arrive(copies)
 
-    def down_tile(c, carry):
-        first = pl.multiple_of(c * 256, 256)
-        hidden = jnp.concatenate([hid_all[i, :, :1728] for i in range(N_GRP)], axis=0)
-        wide[:, pl.ds(first, 256)] = jnp.dot(
-            hidden, w_down[:, pl.ds(first, 256)], preferred_element_type=f32
-        )
-        return carry
-
-    lax.fori_loop(0, DEPTH // 256, down_tile, 0)
-    down_sum = scatter_features(9, down_send, down_recv)
+    hidden = jnp.concatenate([hid_all[i, :, :1728] for i in range(N_GRP)], axis=0)
+    down_sum = scatter_features(9, hidden, w_down, down_send, down_recv)
     final = (residual + down_sum).astype(bf16)
     row_i = lax.broadcasted_iota(jnp.int32, (ROWS, ROWS), 0)
     col_i = lax.broadcasted_iota(jnp.int32, (ROWS, ROWS), 1)
@@ -694,8 +746,8 @@
             pltpu.VMEM((GROWS, KV_HEADS * HEAD_DIM), bf16),
             pltpu.VMEM((GROWS, KV_HEADS * HEAD_DIM), bf16),
             pltpu.VMEM((N_SEQ, REQ_GRP * QROWS, 2 * HEAD_DIM), bf16),
-            pltpu.VMEM((N_SEQ, 96, 128), bf16),
-            pltpu.VMEM((N_SEQ, 96, 128), bf16),
+            pltpu.VMEM((2, N_SEQ, 48, 128), bf16),
+            pltpu.VMEM((2, N_SEQ, 48, 128), bf16),
             pltpu.VMEM((N_GRP, GROWS, GROUP_Q * HEAD_DIM), bf16),
             pltpu.VMEM((ROWS, DEPTH + 128), f32),
             pltpu.VMEM((N_SEQ, 80, 128), bf16),
@@ -711,8 +763,8 @@
             pltpu.VMEM((ROWS, FEAT_PAD), f32),
             pltpu.VMEM((8, FEAT_PAD), f32),
             pltpu.SemaphoreType.DMA((7,)),
-            pltpu.SemaphoreType.DMA((11, N_SEQ)),
-            pltpu.SemaphoreType.DMA((11, N_SEQ)),
+            pltpu.SemaphoreType.DMA((12, N_SEQ)),
+            pltpu.SemaphoreType.DMA((12, N_SEQ)),
         ],
         compiler_params=pltpu.CompilerParams(
             collective_id=0, has_side_effects=True, vmem_limit_bytes=56 * 2**20

time: 76.3 us -> 78.5 us (1.029)
  Pallas kernels: 74.7 us -> 76.9 us
    pallas_call x1, Pallas kernels: 74.7 us -> 76.9 us  [fused_body(): pl.pallas_call(fused_kernel, out_shape=jax.ShapeDtypeStruct(tokens.shape,...]
where the time goes in v3:
time: 78.5 us; the launch traced here: 78.3 us
  Pallas kernels  76.9 us (98%)
  local copies, waits for them, and re-layouts  1.39 us (2%)
    pallas_call x1, Pallas kernels, fused_body(): pl.pallas_call(fused_kernel, out_shape=jax.ShapeDtypeStruct(tokens.shape,...  76.9 us

profile of v3, /device:TPU:0, one launch (start us, length us, event | category | flops | bytes accessed | tf_op | source)
XLA Modules:
  0.0 78.3 jit_solution(2143470631166416041)
XLA Ops:
  0.0 76.9 %shard_map.136 = bf16[16,4,160]{2,1,0:T(4,128)(2,1)} custom-call(s32[16]{0:T(128)} %lengths.1, s32[16]{0:T(128)} %group_perm.1, s32[16,64]{1,0:T(8,128)} %page_table.1, bf16[16,4,160]{2,1,0:T(4,128)(2,1)} %tokens.1, f32[1,160]{1,0:T(1,128)} %bitcast.6, f32[896]{0:T(1024)} %qkv_bias.1, f32[1,160]{1,0:T(1,128)} %bitcast.7, bf16[32,128,1024]{2,1,0:T(8,128)(2,1)} %k_hbm.1, ...), custom_call_target="tpu_custom_call" | custom-call | tf_op jit(solution)/shard_map/pallas_call | solution.py:726
  76.9 1.4 %copy.16 = bf16[16,4,160]{2,1,0:T(4,128)(2,1)} copy(bf16[16,4,160]{2,1,0:T(4,128)(2,1)} %shard_map.136) | data formatting | bytes 40960

commit v4 on v2

--- a/solution.py
+++ b/solution.py
@@ -294,10 +294,8 @@
     o_send,
     o_recv,
     mid_all,
-    gate_send,
-    gate_recv,
-    up_send,
-    up_recv,
+    ff_send,
+    ff_recv,
     hid_all,
     down_send,
     down_recv,
@@ -361,6 +359,7 @@
     started = []
 
     padded[...] = jnp.zeros_like(padded)
+    wide[...] = jnp.zeros_like(wide)
     for i in range(ROWS // STEPS):
         padded[i * STEPS : (i + 1) * STEPS, :FEAT] = tokens[group_perm[i]].astype(f32)
     gains[...] = jnp.zeros_like(gains)
@@ -557,82 +556,100 @@
 
     feature = lax.broadcasted_iota(jnp.int32, (ROWS, FEAT_PAD), 1) < FEAT
 
-    def scatter_features(stage, send, recv):
+    def scatter_features(stage, rows, weight, send, recv):
+        def copy_of(i, source):
+            return pltpu.make_async_remote_copy(
+                src_ref=send.at[i],
+                dst_ref=recv.at[source],
+                send_sem=send_sem.at[stage, i],
+                recv_sem=recv_sem.at[stage, source],
+                device_id={"seq": i},
+                device_id_type=MESH,
+            )
+
+        depth = weight.shape[0] // len(rows)
+        parts = [
+            (((0, 384), (896, DEPTH)), (0, 7, 1, 6)),
+            (((384, 896),), (2, 5, 3, 4)),
+        ]
+        for pieces, peers in parts:
+            for begin, end in pieces:
+                wide[:, begin:end] = sum(
+                    jnp.dot(rows[n], weight[n * depth : (n + 1) * depth, begin:end],
+                            preferred_element_type=f32)
+                    for n in range(len(rows))
+                )
+            for i in peers:
+                first = i * FEAT // 128 * 128
+                window = wide[:, first : first + 384]
+                if i * FEAT - first:
+                    window = pltpu.roll(window, 384 - (i * FEAT - first), 1)
+                send[i] = pack(jnp.where(feature, window[:, :FEAT_PAD], 0.0), 4)
+
+                @pl.when(s != i)
+                def _(i=i):
+                    copy_of(i, s).start()
+
+        recv[s] = send[s]
         for i in range(N_SEQ):
-            first = i * FEAT // 128 * 128
-            window = wide[:, first : first + 384]
-            if i * FEAT - first:
-                window = pltpu.roll(window, 384 - (i * FEAT - first), 1)
-            send[i] = pack(jnp.where(feature, window[:, :FEAT_PAD], 0.0), 4)
-        copies = exchange(stage, "seq", lambda peer: send.at[peer], recv.at[s])
-        started.extend(copies)
-        recv[s] = send[s]
-        arrive(copies)
+
+            @pl.when(s != i)
+            def _(i=i):
+                copy_of(i, i).wait_recv()
+                copy_of(i, i).wait_send()
+
         return unpack(sum(recv[i].astype(f32) for i in range(N_SEQ)), 4)
 
     columns_in = jnp.concatenate([att_all[i] for i in range(N_GRP)], axis=0)
-    wide[:, DEPTH:] = jnp.zeros((ROWS, 128), f32)
-    wide[:, :DEPTH] = jnp.dot(columns_in, w_o[...], preferred_element_type=f32)
-    attn_sum = scatter_features(5, o_send, o_recv)
+    attn_sum = scatter_features(5, [columns_in], w_o, o_send, o_recv)
     residual = sorted_rows + attn_sum
     mid_all[s] = feature_block(residual, gains[1:2, :])
     squares_mid = gather_features(6, mid_all)
 
-    stats = stat_lanes(split_bf16(squares_mid, 2), ROWS).astype(bf16)
-    for i in range(N_GRP):
-        gate_send[i, :, 1792:] = stats[i * GROWS : (i + 1) * GROWS]
-
-    def project(weight, send):
-        def ff_tile(c, carry):
-            first = pl.multiple_of(c * 256, 256)
-            tile = lax.dot_general(
-                x_bf[...], weight[pl.ds(first, 256), :], contract_last, preferred_element_type=f32
-            ).astype(bf16)
-            for i in range(N_GRP):
-                send[i, :, pl.ds(first, 256)] = tile[i * GROWS : (i + 1) * GROWS]
-            return carry
-
-        lax.fori_loop(0, 6, ff_tile, 0)
-        tile = lax.dot_general(
-            x_bf[...], weight[1536:1728, :], contract_last, preferred_element_type=f32
+    stats = stat_lanes(split_bf16(squares_mid, 2), ROWS)
+    stats = jnp.concatenate([stats, stats], axis=0).T[:16].astype(bf16)
+    wide_x = x_wide[:, :DEPTH]
+    gate_x = jnp.concatenate([wide_x, jnp.zeros_like(wide_x)], axis=0).T
+    up_x = pltpu.roll(gate_x, ROWS, 1).astype(bf16)
+    gate_x = gate_x.astype(bf16)
+    units = w_gate.shape[0] // N_GRP
+    loads[4].wait()
+    loads[5].wait()
+    copies = []
+    for d in (2, 3, 1, 0):
+        peer = lax.rem(g + d, N_GRP)
+        rows = pl.ds(pl.multiple_of(peer * units, 16), units)
+        part = jnp.dot(w_gate[rows, :], gate_x, preferred_element_type=f32) + jnp.dot(
+            w_up[rows, :], up_x, preferred_element_type=f32
         )
-        tile = jnp.concatenate([tile, jnp.zeros((ROWS, 64), f32)], axis=1).astype(bf16)
-        for i in range(N_GRP):
-            send[i, :, 1536:1792] = tile[i * GROWS : (i + 1) * GROWS]
-
-    loads[4].wait()
-    project(w_gate, gate_send)
-    gate_copies = exchange(7, "grp", lambda peer: gate_send.at[peer], gate_recv.at[g])
-    started.extend(gate_copies)
-    loads[5].wait()
-    project(w_up, up_send)
-    up_copies = exchange(10, "grp", lambda peer: up_send.at[peer], up_recv.at[g])
-    started.extend(up_copies)
-    gate_recv[g] = gate_send[g]
-    up_recv[g] = up_send[g]
-    arrive(gate_copies)
-    stat = sum(gate_recv[i, :, 1792:].astype(f32) for i in range(N_GRP))
-    scale = lax.rsqrt(jnp.sum(stat, axis=1, keepdims=True) / D + EPSILON)
-    gate = sum(gate_recv[i, :, :1792].astype(f32) for i in range(N_GRP)) * scale
-    gate = gate / (1.0 + jnp.exp(-gate))
-    arrive(up_copies)
-    up = sum(up_recv[i].astype(f32) for i in range(N_GRP)) * scale
-    hid_all[g] = (gate * up).astype(bf16)
+        ff_send[peer, :units] = part.astype(bf16)
+        ff_send[peer, units:] = stats
+        if d:
+            copy = pltpu.make_async_remote_copy(
+                src_ref=ff_send.at[peer],
+                dst_ref=ff_recv.at[g],
+                send_sem=send_sem.at[7, d],
+                recv_sem=recv_sem.at[7, d],
+                device_id={"grp": peer},
+                device_id_type=MESH,
+            )
+            copy.start()
+            copies.append(copy)
+    started.extend(copies)
+    ff_recv[g] = ff_send[g]
+    arrive(copies)
+    summed = sum(ff_recv[i].astype(f32) for i in range(N_GRP))
+    scale = lax.rsqrt((summed[units : units + 1] + summed[units + 1 : units + 2]) / D + EPSILON)
+    summed = summed[:units] * scale
+    hidden = summed / (1.0 + jnp.exp(-summed)) * pltpu.roll(summed, ROWS, 1)
+    hidden = jnp.concatenate([hidden, jnp.zeros((512 - units, 128), f32)], axis=0)
+    hid_all[g] = hidden.T[:ROWS].astype(bf16)
     copies = exchange(8, "grp", lambda peer: hid_all.at[g], hid_all.at[g])
     started.extend(copies)
     loads[6].wait()
     arrive(copies)
-
-    def down_tile(c, carry):
-        first = pl.multiple_of(c * 256, 256)
-        hidden = jnp.concatenate([hid_all[i, :, :1728] for i in range(N_GRP)], axis=0)
-        wide[:, pl.ds(first, 256)] = jnp.dot(
-            hidden, w_down[:, pl.ds(first, 256)], preferred_element_type=f32
-        )
-        return carry
-
-    lax.fori_loop(0, DEPTH // 256, down_tile, 0)
-    down_sum = scatter_features(9, down_send, down_recv)
+    hidden = [hid_all[i, :, :units] for i in range(N_GRP)]
+    down_sum = scatter_features(9, hidden, w_down, down_send, down_recv)
     final = (residual + down_sum).astype(bf16)
     row_i = lax.broadcasted_iota(jnp.int32, (ROWS, ROWS), 0)
     col_i = lax.broadcasted_iota(jnp.int32, (ROWS, ROWS), 1)
@@ -701,11 +718,9 @@
             pltpu.VMEM((N_SEQ, 80, 128), bf16),
             pltpu.VMEM((N_SEQ, 80, 128), bf16),
             pltpu.VMEM((N_SEQ, 96, 128), bf16),
-            pltpu.VMEM((N_GRP, GROWS, 1920), bf16),
-            pltpu.VMEM((N_GRP, GROWS, 1920), bf16),
-            pltpu.VMEM((N_GRP, GROWS, 1792), bf16),
-            pltpu.VMEM((N_GRP, GROWS, 1792), bf16),
-            pltpu.VMEM((N_GRP, GROWS, 1792), bf16),
+            pltpu.VMEM((N_GRP, gate_rows.shape[0] // N_GRP + 16, 128), bf16),
+            pltpu.VMEM((N_GRP, gate_rows.shape[0] // N_GRP + 16, 128), bf16),
+            pltpu.VMEM((N_GRP, ROWS, 512), bf16),
             pltpu.VMEM((N_SEQ, 80, 128), bf16),
             pltpu.VMEM((N_SEQ, 80, 128), bf16),
             pltpu.VMEM((ROWS, FEAT_PAD), f32),

time: 76.3 us -> 75.3 us (0.987)
  Pallas kernels: 74.7 us -> 73.5 us
    pallas_call x1, Pallas kernels: 74.7 us -> 73.5 us  [fused_body(): pl.pallas_call(fused_kernel, out_shape=jax.ShapeDtypeStruct(tokens.shape,...]
where the time goes in v4:
time: 75.3 us; the launch traced here: 74.9 us
  Pallas kernels  73.5 us (98%)
  local copies, waits for them, and re-layouts  1.39 us (2%)
    pallas_call x1, Pallas kernels, fused_body(): pl.pallas_call(fused_kernel, out_shape=jax.ShapeDtypeStruct(tokens.shape,...  73.5 us

profile of v4, /device:TPU:0, one launch (start us, length us, event | category | flops | bytes accessed | tf_op | source)
XLA Modules:
  0.0 74.9 jit_solution(13051095535367564999)
XLA Ops:
  0.0 73.5 %shard_map.136 = bf16[16,4,160]{2,1,0:T(4,128)(2,1)} custom-call(s32[16]{0:T(128)} %lengths.1, s32[16]{0:T(128)} %group_perm.1, s32[16,64]{1,0:T(8,128)} %page_table.1, bf16[16,4,160]{2,1,0:T(4,128)(2,1)} %tokens.1, f32[1,160]{1,0:T(1,128)} %bitcast.6, f32[896]{0:T(1024)} %qkv_bias.1, f32[1,160]{1,0:T(1,128)} %bitcast.7, bf16[32,128,1024]{2,1,0:T(8,128)(2,1)} %k_hbm.1, ...), custom_call_target="tpu_custom_call" | custom-call | tf_op jit(solution)/shard_map/pallas_call | solution.py:691
  73.6 1.4 %copy.16 = bf16[16,4,160]{2,1,0:T(4,128)(2,1)} copy(bf16[16,4,160]{2,1,0:T(4,128)(2,1)} %shard_map.136) | data formatting | bytes 40960

commit v5 on v4

--- a/solution.py
+++ b/solution.py
@@ -323,8 +323,7 @@
             ]
         )
     ]
-    for load in loads:
-        load.start()
+    loads[0].start()
     barrier = pltpu.get_barrier_semaphore()
     for d in range(1, N_SEQ):
         pl.semaphore_signal(
@@ -379,6 +378,8 @@
     def gather_features(stage, blocks):
         copies = exchange(stage, "seq", lambda peer: blocks.at[s], blocks.at[s])
         started.extend(copies)
+        if stage == 0:
+            loads[1].start()
         arrive(copies)
         lane = lax.broadcasted_iota(jnp.int32, (ROWS, FEAT_PAD), 1)
         x_wide[...] = jnp.zeros_like(x_wide)
@@ -406,6 +407,8 @@
         qkv_send[i, :, 896:] = stats[rows]
     copies = exchange(1, "grp", lambda peer: qkv_send.at[peer], qkv_recv.at[g])
     started.extend(copies)
+    for load in loads[2:]:
+        load.start()
     qkv_recv[g] = qkv_send[g]
 
     row16 = lax.broadcasted_iota(jnp.int32, (GROWS, HEAD_DIM), 0)
@@ -568,27 +571,30 @@
             )
 
         depth = weight.shape[0] // len(rows)
-        parts = [
-            (((0, 384), (896, DEPTH)), (0, 7, 1, 6)),
-            (((384, 896),), (2, 5, 3, 4)),
-        ]
-        for pieces, peers in parts:
-            for begin, end in pieces:
-                wide[:, begin:end] = sum(
-                    jnp.dot(rows[n], weight[n * depth : (n + 1) * depth, begin:end],
-                            preferred_element_type=f32)
-                    for n in range(len(rows))
+
+        def tile(c, carry):
+            lanes = pl.ds(pl.multiple_of(c * 256, 256), 256)
+            wide[:, lanes] = sum(
+                jnp.dot(
+                    rows[n][...],
+                    weight[n * depth : (n + 1) * depth, lanes],
+                    preferred_element_type=f32,
                 )
-            for i in peers:
-                first = i * FEAT // 128 * 128
-                window = wide[:, first : first + 384]
-                if i * FEAT - first:
-                    window = pltpu.roll(window, 384 - (i * FEAT - first), 1)
-                send[i] = pack(jnp.where(feature, window[:, :FEAT_PAD], 0.0), 4)
-
-                @pl.when(s != i)
-                def _(i=i):
-                    copy_of(i, s).start()
+                for n in range(len(rows))
+            )
+            return carry
+
+        lax.fori_loop(0, DEPTH // 256, tile, 0)
+        for i in (0, 7, 1, 6, 2, 5, 3, 4):
+            first = i * FEAT // 128 * 128
+            window = wide[:, first : first + 384]
+            if i * FEAT - first:
+                window = pltpu.roll(window, 384 - (i * FEAT - first), 1)
+            send[i] = pack(jnp.where(feature, window[:, :FEAT_PAD], 0.0), 4)
+
+            @pl.when(s != i)
+            def _(i=i):
+                copy_of(i, s).start()
 
         recv[s] = send[s]
         for i in range(N_SEQ):
@@ -615,8 +621,18 @@
     units = w_gate.shape[0] // N_GRP
     loads[4].wait()
     loads[5].wait()
-    copies = []
-    for d in (2, 3, 1, 0):
+
+    def ff_copy(d):
+        return pltpu.make_async_remote_copy(
+            src_ref=ff_send.at[lax.rem(g + d, N_GRP)],
+            dst_ref=ff_recv.at[g],
+            send_sem=send_sem.at[7, d],
+            recv_sem=recv_sem.at[7, d],
+            device_id={"grp": lax.rem(g + d, N_GRP)},
+            device_id_type=MESH,
+        )
+
+    def ff_units(d, carry):
         peer = lax.rem(g + d, N_GRP)
         rows = pl.ds(pl.multiple_of(peer * units, 16), units)
         part = jnp.dot(w_gate[rows, :], gate_x, preferred_element_type=f32) + jnp.dot(
@@ -624,17 +640,15 @@
         )
         ff_send[peer, :units] = part.astype(bf16)
         ff_send[peer, units:] = stats
-        if d:
-            copy = pltpu.make_async_remote_copy(
-                src_ref=ff_send.at[peer],
-                dst_ref=ff_recv.at[g],
-                send_sem=send_sem.at[7, d],
-                recv_sem=recv_sem.at[7, d],
-                device_id={"grp": peer},
-                device_id_type=MESH,
-            )
-            copy.start()
-            copies.append(copy)
+
+        @pl.when(d < N_GRP)
+        def _():
+            ff_copy(d).start()
+
+        return carry
+
+    lax.fori_loop(1, N_GRP + 1, ff_units, 0)
+    copies = [ff_copy(d) for d in range(1, N_GRP)]
     started.extend(copies)
     ff_recv[g] = ff_send[g]
     arrive(copies)

time: 75.3 us -> 75.3 us (level)
  no operation moved by 1% of the time
where the time goes in v5:
time: 75.3 us; the launch traced here: 74.8 us
  Pallas kernels  73.4 us (97%)
  local copies, waits for them, and re-layouts  1.39 us (2%)
    pallas_call x1, Pallas kernels, fused_body(): pl.pallas_call(fused_kernel, out_shape=jax.ShapeDtypeStruct(tokens.shape,...  73.4 us

profile of v5, /device:TPU:0, one launch (start us, length us, event | category | flops | bytes accessed | tf_op | source)
XLA Modules:
  0.0 74.8 jit_solution(7395259674993413201)
XLA Ops:
  0.0 73.4 %shard_map.136 = bf16[16,4,160]{2,1,0:T(4,128)(2,1)} custom-call(s32[16]{0:T(128)} %lengths.1, s32[16]{0:T(128)} %group_perm.1, s32[16,64]{1,0:T(8,128)} %page_table.1, bf16[16,4,160]{2,1,0:T(4,128)(2,1)} %tokens.1, f32[1,160]{1,0:T(1,128)} %bitcast.6, f32[896]{0:T(1024)} %qkv_bias.1, f32[1,160]{1,0:T(1,128)} %bitcast.7, bf16[32,128,1024]{2,1,0:T(8,128)(2,1)} %k_hbm.1, ...), custom_call_target="tpu_custom_call" | custom-call | tf_op jit(solution)/shard_map/pallas_call | solution.py:705
  73.4 1.4 %copy.16 = bf16[16,4,160]{2,1,0:T(4,128)(2,1)} copy(bf16[16,4,160]{2,1,0:T(4,128)(2,1)} %shard_map.136) | data formatting | bytes 40960

commit v6 on v5

--- a/solution.py
+++ b/solution.py
@@ -436,12 +436,6 @@
     copies = exchange(2, "seq", lambda peer: heads_all.at[s], heads_all.at[s])
     started.extend(copies)
     q_pairs[...] = jnp.zeros_like(q_pairs)
-    arrive(copies)
-
-    def head(h):
-        lane = (h % per_dev) * HEAD_DIM
-        return heads_all[h // per_dev, :, lane : lane + HEAD_DIM]
-
     n_q = REQ_GRP * QROWS
     spread_row = lax.broadcasted_iota(jnp.int32, (n_q, GROUP_Q * GROWS), 0)
     spread_col = lax.broadcasted_iota(jnp.int32, (n_q, GROUP_Q * GROWS), 1)
@@ -450,6 +444,27 @@
         & (spread_row % QROWS // STEPS == spread_col // GROWS)
         & (spread_row % STEPS == spread_col % STEPS)
     ).astype(f32).astype(bf16)
+    pick_row = lax.broadcasted_iota(jnp.int32, (GROUP_Q * GROWS, n_q), 0)
+    pick_col = lax.broadcasted_iota(jnp.int32, (GROUP_Q * GROWS, n_q), 1)
+    pick = (
+        (pick_col // QROWS == pick_row % GROWS // STEPS)
+        & (pick_col % QROWS // STEPS == pick_row // GROWS)
+        & (pick_col % STEPS == pick_row % STEPS)
+    ).astype(f32).astype(bf16)
+    row_i = lax.broadcasted_iota(jnp.int32, (ROWS, ROWS), 0)
+    col_i = lax.broadcasted_iota(jnp.int32, (ROWS, ROWS), 1)
+    origin = jnp.zeros((ROWS, ROWS), jnp.int32)
+    for i in range(ROWS // STEPS):
+        origin = jnp.where(col_i // STEPS == i, group_perm[i], origin)
+    back = (
+        ((row_i // STEPS) == origin) & ((col_i % STEPS) == (row_i % STEPS))
+    ).astype(f32).astype(bf16)
+    arrive(copies)
+
+    def head(h):
+        lane = (h % per_dev) * HEAD_DIM
+        return heads_all[h // per_dev, :, lane : lane + HEAD_DIM]
+
     for k in range(KV_HEADS):
         stacked = jnp.concatenate([head(k * GROUP_Q + j) for j in range(GROUP_Q)], axis=0)
         placed = jnp.dot(spread, stacked, preferred_element_type=f32).astype(bf16)
@@ -514,13 +529,6 @@
         return carry
 
     lax.fori_loop(0, REQ_GRP, attend, 0)
-    pick_row = lax.broadcasted_iota(jnp.int32, (GROUP_Q * GROWS, n_q), 0)
-    pick_col = lax.broadcasted_iota(jnp.int32, (GROUP_Q * GROWS, n_q), 1)
-    pick = (
-        (pick_col // QROWS == pick_row % GROWS // STEPS)
-        & (pick_col % QROWS // STEPS == pick_row // GROWS)
-        & (pick_col % STEPS == pick_row % STEPS)
-    ).astype(f32).astype(bf16)
     n_out = GROUP_Q * GROWS
     for k in range(KV_HEADS):
         picked = jnp.dot(pick, att_held[k], preferred_element_type=f32)
@@ -665,14 +673,6 @@
     hidden = [hid_all[i, :, :units] for i in range(N_GRP)]
     down_sum = scatter_features(9, hidden, w_down, down_send, down_recv)
     final = (residual + down_sum).astype(bf16)
-    row_i = lax.broadcasted_iota(jnp.int32, (ROWS, ROWS), 0)
-    col_i = lax.broadcasted_iota(jnp.int32, (ROWS, ROWS), 1)
-    origin = jnp.zeros((ROWS, ROWS), jnp.int32)
-    for i in range(ROWS // STEPS):
-        origin = jnp.where(col_i // STEPS == i, group_perm[i], origin)
-    back = (
-        ((row_i // STEPS) == origin) & ((col_i % STEPS) == (row_i % STEPS))
-    ).astype(f32).astype(bf16)
     ordered = jnp.dot(back, final, preferred_element_type=f32)
     for i in range(ROWS // STEPS):
         out[i] = ordered[i * STEPS : (i + 1) * STEPS, :FEAT].astype(bf16)

time: 75.3 us -> 75.3 us (level)
  no operation moved by 1% of the time
where the time goes in v6:
time: 75.3 us; the launch traced here: 74.8 us
  Pallas kernels  73.4 us (97%)
  local copies, waits for them, and re-layouts  1.39 us (2%)
    pallas_call x1, Pallas kernels, fused_body(): pl.pallas_call(fused_kernel, out_shape=jax.ShapeDtypeStruct(tokens.shape,...  73.4 us

profile of v6, /device:TPU:0, one launch (start us, length us, event | category | flops | bytes accessed | tf_op | source)
XLA Modules:
  0.0 74.8 jit_solution(7240938811312868204)
XLA Ops:
  0.0 73.4 %shard_map.136 = bf16[16,4,160]{2,1,0:T(4,128)(2,1)} custom-call(s32[16]{0:T(128)} %lengths.1, s32[16]{0:T(128)} %group_perm.1, s32[16,64]{1,0:T(8,128)} %page_table.1, bf16[16,4,160]{2,1,0:T(4,128)(2,1)} %tokens.1, f32[1,160]{1,0:T(1,128)} %bitcast.6, f32[896]{0:T(1024)} %qkv_bias.1, f32[1,160]{1,0:T(1,128)} %bitcast.7, bf16[32,128,1024]{2,1,0:T(8,128)(2,1)} %k_hbm.1, ...), custom_call_target="tpu_custom_call" | custom-call | tf_op jit(solution)/shard_map/pallas_call | solution.py:705
  73.4 1.4 %copy.16 = bf16[16,4,160]{2,1,0:T(4,128)(2,1)} copy(bf16[16,4,160]{2,1,0:T(4,128)(2,1)} %shard_map.136) | data formatting | bytes 40960
